TPU v7x, 32 devices: a whole 2x2x4 slice. The times are simulated.
32 devices in a mesh: seq: 8 (over z, x), chan: 4 (over y, core).
Axes of the slice: x: 2, y: 2, z: 4, core: 2. Of those that a mesh axis runs over, the one named last changes fastest.
Arguments:
- projected: bfloat16 [3, 64, 524288], P(None, None, ('seq', 'chan')), may hold values from -6 to 6
- live_blocks: int32 [4096], P('seq'), may hold values 0 or 1
- filters: float32 [4, 524288], P('chan', 'seq'), as said below
- skip_gain: float32 [64], P('chan'), may hold values from -2 to 2
Outputs:
- gated: bfloat16 [64, 524288], P('chan', 'seq')
Inputs may be any that keep to these rules, and one draw needn't show every extreme that they name: filters holds finite float32 taps.
All inputs are finite; a program needn't handle non-finite values. No bound on the sum of `live_blocks` on one device may be relied on, other than what follows from the above.
Results may differ from a plain program's by a relative error of at most 0.0049.
Values may be sent and summed in bfloat16 or wider, within the bound.
A program may use at most 256 MiB of HBM per device.

v0:
```python
from functools import partial
import math

import jax
import jax.numpy as jnp
from jax import lax
from jax.sharding import PartitionSpec as P

P_SIZE = 128
Q = 64
R = 128
N = 1048576


def unit_root(exponent, total):
    angles = 2.0 * math.pi / total * exponent.astype(jnp.float32)
    return (jnp.cos(angles), -jnp.sin(angles))


def rotate(real_part, imag_part, cos_part, sin_part):
    return (
        real_part * cos_part - imag_part * sin_part,
        real_part * sin_part + imag_part * cos_part,
    )


def dft_apply(form, mat_real, mat_imag, real_part, imag_part):
    product = partial(jnp.einsum, form, precision=lax.Precision.HIGHEST)
    if imag_part is None:
        return (product(mat_real, real_part), product(mat_imag, real_part))
    first = product(mat_real, real_part) - product(mat_imag, imag_part)
    second = product(mat_real, imag_part) + product(mat_imag, real_part)
    return (first, second)


def early_sections(real_part, imag_part, tables):
    first_real, first_imag, twist_cos, twist_sin, second_real, second_imag, outer_cos, outer_sin = (
        tables
    )
    real_part, imag_part = dft_apply("kn,cnqr->ckqr", first_real, first_imag, real_part, imag_part)
    real_part, imag_part = rotate(real_part, imag_part, twist_cos, twist_sin)
    real_part, imag_part = dft_apply(
        "kn,cpnr->cpkr", second_real, second_imag, real_part, imag_part
    )
    real_part, imag_part = rotate(real_part, imag_part, outer_cos, outer_sin)
    width_now = real_part.shape[0]
    narrow = real_part.shape[3]
    return (
        real_part.reshape(width_now, P_SIZE * Q, narrow),
        imag_part.reshape(width_now, P_SIZE * Q, narrow),
    )


def body(projected, live_blocks, filters, skip_gain):
    seq_index = lax.axis_index("seq")
    blocks = live_blocks.shape[0]
    span = blocks * R
    moved = lax.all_to_all(projected, "chan", split_axis=1, concat_axis=2, tiled=True)
    keep_rows = (
        jnp.broadcast_to(live_blocks[:, None], (blocks, R)).reshape(span).astype(jnp.float32)
    )
    gate_rows = moved[0]
    product_rows = (
        moved[1].astype(jnp.float32) * moved[2].astype(jnp.float32) * keep_rows[None, :]
    ).astype(jnp.bfloat16)
    channels = product_rows.shape[0]
    local_groups = filters.shape[0]
    half_p = P_SIZE // 2
    columns = lax.all_to_all(
        product_rows.reshape(channels, blocks, R), "seq", split_axis=2, concat_axis=1, tiled=True
    )
    narrow = columns.shape[2]
    filter_cols = lax.all_to_all(
        filters.reshape(local_groups, blocks, R), "seq", split_axis=2, concat_axis=1, tiled=True
    )
    filter_signal = filter_cols.reshape(local_groups, half_p, Q, narrow)
    signal = columns.astype(jnp.float32).reshape(channels, half_p, Q, narrow)
    real_part, imag_part = (signal, None)
    width_now = real_part.shape[0]
    first_k = jnp.arange(P_SIZE, dtype=jnp.int32)
    first_n = jnp.arange(half_p, dtype=jnp.int32)
    first_real, first_imag = unit_root(first_k[:, None] * first_n[None, :] % P_SIZE, P_SIZE)
    second_k = jnp.arange(Q, dtype=jnp.int32)
    twist_cos, twist_sin = unit_root(
        first_k[:, None] * second_k[None, :] % (P_SIZE * Q), P_SIZE * Q
    )
    twist_cos, twist_sin = (twist_cos[:, :, None], twist_sin[:, :, None])
    second_real, second_imag = unit_root(second_k[:, None] * second_k[None, :] % Q, Q)
    depth = seq_index * narrow + jnp.arange(narrow, dtype=jnp.int32)[None, None, :]
    joined = first_k[:, None, None] + P_SIZE * second_k[None, :, None]
    outer_cos, outer_sin = unit_root(joined * depth % N, N)
    tables = (
        first_real,
        first_imag,
        twist_cos,
        twist_sin,
        second_real,
        second_imag,
        outer_cos,
        outer_sin,
    )
    real_part, imag_part = early_sections(real_part, imag_part, tables)
    real_part, imag_part = (
        lax.all_to_all(real_part, "seq", split_axis=1, concat_axis=2, tiled=True),
        lax.all_to_all(imag_part, "seq", split_axis=1, concat_axis=2, tiled=True),
    )
    freq_rows = real_part.shape[1]
    filt_real, filt_imag = early_sections(filter_signal, None, tables)
    filt_real, filt_imag = (
        lax.all_to_all(filt_real, "seq", split_axis=1, concat_axis=2, tiled=True),
        lax.all_to_all(filt_imag, "seq", split_axis=1, concat_axis=2, tiled=True),
    )
    third_k = jnp.arange(R, dtype=jnp.int32)
    third_real, third_imag = unit_root(third_k[:, None] * third_k[None, :] % R, R)
    real_part, imag_part = dft_apply("kn,cfn->cfk", third_real, third_imag, real_part, imag_part)
    filt_real, filt_imag = dft_apply("kn,cfn->cfk", third_real, third_imag, filt_real, filt_imag)
    filt_real = filt_real[:, None]
    filt_imag = filt_imag[:, None]
    grouped_shape = (local_groups, width_now // local_groups, freq_rows, R)
    real_part, imag_part = rotate(
        real_part.reshape(grouped_shape), imag_part.reshape(grouped_shape), filt_real, filt_imag
    )
    real_part = real_part.reshape(width_now, freq_rows, R)
    imag_part = imag_part.reshape(width_now, freq_rows, R)
    real_part, imag_part = dft_apply("kn,cfn->cfk", third_real, -third_imag, real_part, imag_part)
    real_part, imag_part = (
        lax.all_to_all(real_part, "seq", split_axis=2, concat_axis=1, tiled=True),
        lax.all_to_all(imag_part, "seq", split_axis=2, concat_axis=1, tiled=True),
    )
    real_part = real_part.reshape(width_now, P_SIZE, Q, narrow)
    imag_part = imag_part.reshape(width_now, P_SIZE, Q, narrow)
    real_part, imag_part = rotate(real_part, imag_part, outer_cos, -outer_sin)
    real_part, imag_part = dft_apply(
        "kn,cpnr->cpkr", second_real, -second_imag, real_part, imag_part
    )
    real_part, imag_part = rotate(real_part, imag_part, twist_cos, -twist_sin)
    back_real = first_real.T
    back_imag = -first_imag.T
    product = partial(jnp.einsum, "nk,ckqr->cnqr", precision=lax.Precision.HIGHEST)
    spatial = (product(back_real, real_part) - product(back_imag, imag_part)).reshape(
        channels, half_p * Q, narrow
    )
    spatial = spatial * (1.0 / N)
    convolved = lax.all_to_all(spatial, "seq", split_axis=1, concat_axis=2, tiled=True).reshape(
        channels, span
    )
    direct = skip_gain[:, None] * product_rows.astype(jnp.float32)
    return (gate_rows.astype(jnp.float32) * (convolved + direct)).astype(jnp.bfloat16)


def solution(mesh):
    in_specs = (P(None, None, ("seq", "chan")), P("seq"), P("chan", "seq"), P("chan"))
    out_specs = P("chan", "seq")
    return jax.shard_map(body, mesh=mesh, in_specs=in_specs, out_specs=out_specs, check_vma=False)
```

profile of v0, /device:TPU:0, one launch (start us, length us, event | category | flops | bytes accessed | tf_op | source)
XLA Modules:
  0.0 1804.5 jit_solution(7718523280327403817)
XLA Ops:
  18.1 93.0 %all-to-all-done = bf16[3,64,16384]{2,0,1:T(4,128)(2,1)} async-done(((bf16[3,64,16384]{2,0,1:T(4,128)(2,1)}), bf16[3,64,16384]{2,0,1:T(4,128)(2,1)}, u32[]{:S(2)}, u32[]{:S(2)}) %all-to-all-start) | async-done | bytes 6291488 | tf_op jit(solution)/shard_map/all_to_all | solution.py:58
  170.5 38.6 %reduce = f32[8192,16]{1,0:T(8,128)} reduce(f32[8192,1,16]{2,1,0:T(1,128)} %bitcast.264, f32[]{:T(128)} %broadcast.426), dimensions={1}, to_apply=%bitcast.208.reduce_sub_computation | reduce | bytes 1048580
  217.9 38.4 %reduce.2 = f32[8192,16]{1,0:T(8,128)} reduce(f32[8192,1,16]{2,1,0:T(1,128)} %bitcast.265, f32[]{:T(128)} %broadcast.426), dimensions={1}, to_apply=%bitcast.210.reduce_sub_computation | reduce | bytes 1048580
  339.3 23.9 %fusion = (f32[16,128,64,16]{1,2,3,0:T(8,128)}, f32[16,128,64,16]{1,2,3,0:T(8,128)}) fusion(f32[128,64,16]{0,1,2:T(8,128)S(1)} %get-tuple-element.16, f32[128,64,16]{0,1,2:T(8,128)S(1)} %get-tuple-element.17, f32[16,128,16,64]{1,3,2,0:T(8,128)} %fusion.12, f32[16,128,16,64]{1,3,2,0:T(8,128)} %fusion.14, f32[16,128,16,64]{1,3,2,0:T(8,128)} %fusion.10, ...), kind=kOutput, calls=%fused_computation.2 | convolution fusion | flops 1627447296 | bytes 51380224 | tf_op jit(solution)/shard_map/kn,cpnr->cpkr/dot_general | solution.py:32
  363.3 50.2 %copy.195 = f32[16,128,64,16]{3,0,2,1:T(8,128)} copy(f32[16,128,64,16]{1,2,3,0:T(8,128)} %get-tuple-element.7) | data formatting | bytes 16777216 | tf_op jit(solution)/shard_map/reshape | solution.py:49
  413.4 59.3 %reshape.298 = f32[8,1,262144]{2,1,0:T(1,128)} reshape(f32[8192,16,16]{2,1,0:T(8,128)} %bitcast.214) | data formatting | bytes 16777216
  478.7 50.2 %copy.198 = f32[16,128,64,16]{3,0,2,1:T(8,128)} copy(f32[16,128,64,16]{1,2,3,0:T(8,128)} %get-tuple-element.8) | data formatting | bytes 16777216 | tf_op jit(solution)/shard_map/reshape | solution.py:50
  528.9 59.0 %reshape.296 = f32[8,1,262144]{2,1,0:T(1,128)} reshape(f32[8192,16,16]{2,1,0:T(8,128)} %bitcast.212) | data formatting | bytes 16777216
  587.9 71.6 %all-to-all-done.2 = f32[8,1,262144]{2,1,0:T(1,128)} async-done(((f32[8,1,262144]{2,1,0:T(1,128)}), f32[8,1,262144]{2,1,0:T(1,128)}, u32[]{:S(2)}, u32[]{:S(2)}) %all-to-all-start.2) | async-done | bytes 8388640 | tf_op jit(solution)/shard_map/all_to_all | solution.py:104
  700.4 26.6 %reduce.4 = f32[8,262144]{1,0:T(8,128)} reduce(f32[8,1,262144]{2,1,0:T(1,128)} %all-to-all-done.2, f32[]{:T(128)} %broadcast.426), dimensions={1}, to_apply=%all_to_all.120.reduce_sub_computation | reduce | bytes 16777220 | tf_op jit(solution)/shard_map/all_to_all | solution.py:104
  727.0 51.3 %reshape.299 = f32[8192,16,16]{2,1,0:T(8,128)} reshape(f32[8,262144]{1,0:T(8,128)} %reduce.4) | data formatting | bytes 16777216
  778.3 40.1 %copy.145 = f32[16,1024,8,16]{1,3,2,0:T(8,128)} copy(f32[16,1024,8,16]{3,0,1,2:T(8,128)} %bitcast.22) | data formatting | bytes 16777216 | tf_op jit(solution)/shard_map/all_to_all | solution.py:104
  818.3 17.5 fusion.45
  835.9 16.0 fusion.55
  851.9 26.4 %reduce.5 = f32[8,262144]{1,0:T(8,128)} reduce(f32[8,1,262144]{2,1,0:T(1,128)} %all-to-all-done.3, f32[]{:T(128)} %broadcast.426), dimensions={1}, to_apply=%all_to_all.124.reduce_sub_computation | reduce | bytes 16777220 | tf_op jit(solution)/shard_map/all_to_all | solution.py:105
  878.3 51.2 %reshape.297 = f32[8192,16,16]{2,1,0:T(8,128)} reshape(f32[8,262144]{1,0:T(8,128)} %reduce.5) | data formatting | bytes 16777216
  929.5 40.1 %copy.150 = f32[16,1024,8,16]{1,3,2,0:T(8,128)} copy(f32[16,1024,8,16]{3,0,1,2:T(8,128)} %bitcast.28) | data formatting | bytes 16777216 | tf_op jit(solution)/shard_map/all_to_all | solution.py:105
  969.6 17.4 fusion.47
  987.0 23.8 %multiply_subtract_fusion.1 = (f32[16,1024,128]{2,1,0:T(8,128)}, f32[16,1024,128]{2,1,0:T(8,128)}) fusion(f32[1024,128]{1,0:T(8,128)S(1)} %convolution_add_fusion.1, f32[1024,128]{1,0:T(8,128)S(1)} %convolution_subtract_fusion.1, f32[16,1024,128]{2,1,0:T(8,128)} %fusion.45, f32[16,1024,128]{2,1,0:T(8,128)} %fusion.55, f32[16,1024,128]{2,1,0:T(8,128)} %fusion.47, ...), kind=kOutput, calls=%fused_computation.22 | convolution fusion | flops 3238232064 | bytes 51380224 | tf_op jit(solution)/shard_map/kn,cfn->cfk/dot_general | solution.py:32
  1076.2 151.1 %all-to-all-done.8 = f32[16,1024,128]{1,0,2:T(8,128)} async-done(((f32[16,1024,128]{1,0,2:T(8,128)}), f32[16,1024,128]{1,0,2:T(8,128)}, u32[]{:S(2)}, u32[]{:S(2)}) %all-to-all-start.8) | async-done | bytes 8388640 | tf_op jit(solution)/shard_map/all_to_all | solution.py:128
  1270.2 144.2 %all-to-all-done.7 = f32[16,1024,128]{1,0,2:T(8,128)} async-done(((f32[16,1024,128]{1,0,2:T(8,128)}), f32[16,1024,128]{1,0,2:T(8,128)}, u32[]{:S(2)}, u32[]{:S(2)}) %all-to-all-start.7) | async-done | bytes 8388640 | tf_op jit(solution)/shard_map/all_to_all | solution.py:127
  1452.3 16.7 fusion.20
  1469.0 13.8 fusion.18
  1494.9 19.2 %subtract_bitcast_fusion = (f32[16,128,64,16]{1,2,3,0:T(8,128)}, f32[16,128,64,16]{1,2,3,0:T(8,128)}) fusion(f32[128,64]{0,1:T(8,128)S(1)} %fusion.155, f32[128,64]{0,1:T(8,128)S(1)} %copy-done.10, f32[16,128,16,64]{1,3,2,0:T(8,128)} %fusion.20, f32[16,128,16,64]{1,3,2,0:T(8,128)} %fusion.18, f32[16,128,16,64]{1,3,2,0:T(8,128)} %fusion.19, ...), kind=kOutput, calls=%fused_computation.18 | convolution fusion | flops 1633738752 | bytes 59834368 | tf_op jit(solution)/shard_map/kn,cpnr->cpkr/dot_general | solution.py:31
  1514.2 14.3 fusion.4
  1540.5 26.4 %copy.207 = f32[16,64,64,16]{3,0,2,1:T(8,128)} copy(f32[16,64,64,16]{1,3,2,0:T(8,128)} %multiply_bitcast_fusion) | data formatting | bytes 8388608 | tf_op jit(solution)/shard_map/mul | solution.py:143
  1566.8 18.2 %reshape.300 = f32[8,1,131072]{2,1,0:T(1,128)} reshape(f32[4096,16,16]{2,1,0:T(8,128)} %bitcast.253) | data formatting | bytes 8388608
  1601.2 81.5 %all-to-all-done.9 = f32[8,1,131072]{2,1,0:T(1,128)} async-done(((f32[8,1,131072]{2,1,0:T(1,128)}), f32[8,1,131072]{2,1,0:T(1,128)}, u32[]{:S(2)}, u32[]{:S(2)}) %all-to-all-start.9) | async-done | bytes 4194336 | tf_op jit(solution)/shard_map/all_to_all | solution.py:144
  1682.7 14.2 reduce.6
  1696.9 24.3 %reshape.301 = f32[4096,16,16]{2,1,0:T(8,128)} reshape(f32[8,131072]{1,0:T(8,128)} %reduce.6) | data formatting | bytes 8388608
  1721.2 31.9 %copy.181 = f32[16,512,8,16]{3,2,1,0:T(8,128)} copy(f32[16,512,8,16]{3,0,1,2:T(8,128)} %bitcast.254) | data formatting | bytes 8388608 | tf_op jit(solution)/shard_map/all_to_all | solution.py:144
  1753.1 44.5 %reshape.277 = f32[16,65536]{1,0:T(8,128)} reshape(f32[16,512,8,16]{3,2,1,0:T(8,128)} %copy.181) | data formatting | bytes 8388608 | tf_op jit(solution)/shard_map/reshape | solution.py:144
  (126 shorter events, 409.0 us)
Async XLA Ops:
  11.4 5.8 copy-start.12
  11.4 6.6 copy-start.15
  11.4 99.6 %all-to-all-start = ((bf16[3,64,16384]{2,0,1:T(4,128)(2,1)}), bf16[3,64,16384]{2,0,1:T(4,128)(2,1)}, u32[]{:S(2)}, u32[]{:S(2)}) async-start(bf16[3,64,16384]{2,0,1:T(4,128)(2,1)} %copy.131), calls=%async_computation | async-start | bytes 16777216 | tf_op jit(solution)/shard_map/all_to_all | solution.py:58
  18.1 124.4 %copy-start.13 = (f32[512]{0:T(512)}, f32[512]{0:T(512)S(1)}, u32[]{:S(2)}) copy-start(f32[512]{0:T(512)S(1)} %convert_element_type.167) | copy-start | bytes 6148
  111.1 37.0 %all-to-all-start.4 = ((f32[1,512,128]{1,0,2:T(1,128)}), f32[1,512,128]{1,0,2:T(1,128)S(1)}, u32[]{:S(2)}, u32[]{:S(2)}) async-start(f32[1,512,128]{1,0,2:T(1,128)} %copy.152), calls=%async_computation.4 | async-start | bytes 524288 | tf_op jit(solution)/shard_map/all_to_all | solution.py:73
  148.1 112.6 %all-to-all-start.1 = ((bf16[16,512,128]{1,0,2:T(8,128)(2,1)}), bf16[16,512,128]{1,0,2:T(8,128)(2,1)}, u32[]{:S(2)}, u32[]{:S(2)}) async-start(bf16[16,512,128]{1,0,2:T(8,128)(2,1)} %copy.133), calls=%async_computation.1 | async-start | bytes 4194304 | tf_op jit(solution)/shard_map/all_to_all | solution.py:69
  154.5 15.4 copy-start.11
  154.5 137.4 %copy-start.9 = (f32[128,64]{0,1:T(8,128)}, f32[128,64]{0,1:T(8,128)S(1)}, u32[]{:S(2)}) copy-start(f32[128,64]{0,1:T(8,128)S(1)} %get-tuple-element.18) | copy-start | bytes 98308
  157.7 181.6 %copy-start.6 = (f32[128,64,16]{0,1,2:T(8,128)}, f32[128,64,16]{0,1,2:T(8,128)S(1)}, u32[]{:S(2)}) copy-start(f32[128,64,16]{0,1,2:T(8,128)S(1)} %get-tuple-element.17) | copy-start | bytes 1572868
  260.7 72.4 %all-to-all-start.6 = ((f32[8,1,16384]{2,1,0:T(1,128)}), f32[8,1,16384]{2,1,0:T(1,128)S(1)}, u32[]{:S(2)}, u32[]{:S(2)}) async-start(f32[8,1,16384]{2,1,0:T(1,128)} %reshape.292), calls=%async_computation.6 | async-start | bytes 1048576 | tf_op jit(solution)/shard_map/all_to_all | solution.py:111
  284.3 7.6 copy-start.3
  299.0 22.8 %copy-start.1 = (f32[16,128,64,16]{1,3,2,0:T(8,128)}, f32[16,128,64,16]{1,3,2,0:T(8,128)S(1)}, u32[]{:S(2)}) copy-start(f32[16,128,64,16]{1,3,2,0:T(8,128)S(1)} %get-tuple-element.12) | copy-start | bytes 25165828
  333.1 139.7 %all-to-all-start.5 = ((f32[8,1,16384]{2,1,0:T(1,128)}), f32[8,1,16384]{2,1,0:T(1,128)S(1)}, u32[]{:S(2)}, u32[]{:S(2)}) async-start(f32[8,1,16384]{2,1,0:T(1,128)} %reshape.294), calls=%async_computation.5 | async-start | bytes 1048576 | tf_op jit(solution)/shard_map/all_to_all | solution.py:110
  472.7 186.7 %all-to-all-start.2 = ((f32[8,1,262144]{2,1,0:T(1,128)}), f32[8,1,262144]{2,1,0:T(1,128)}, u32[]{:S(2)}, u32[]{:S(2)}) async-start(f32[8,1,262144]{2,1,0:T(1,128)} %reshape.298), calls=%async_computation.2 | async-start | bytes 16777216 | tf_op jit(solution)/shard_map/all_to_all | solution.py:104
  659.5 192.4 %all-to-all-start.3 = ((f32[8,1,262144]{2,1,0:T(1,128)}), f32[8,1,262144]{2,1,0:T(1,128)}, u32[]{:S(2)}, u32[]{:S(2)}) async-start(f32[8,1,262144]{2,1,0:T(1,128)} %reshape.296), calls=%async_computation.3 | async-start | bytes 16777216 | tf_op jit(solution)/shard_map/all_to_all | solution.py:105
  818.3 17.5 slice-start.2
  818.3 17.5 slice-start.3
  1010.8 10.6 copy-start.2
  1039.8 187.5 %all-to-all-start.8 = ((f32[16,1024,128]{1,0,2:T(8,128)}), f32[16,1024,128]{1,0,2:T(8,128)}, u32[]{:S(2)}, u32[]{:S(2)}) async-start(f32[16,1024,128]{1,0,2:T(8,128)} %copy.170), calls=%async_computation.8 | async-start | bytes 16777216 | tf_op jit(solution)/shard_map/all_to_all | solution.py:128
  1227.3 187.1 %all-to-all-start.7 = ((f32[16,1024,128]{1,0,2:T(8,128)}), f32[16,1024,128]{1,0,2:T(8,128)}, u32[]{:S(2)}, u32[]{:S(2)}) async-start(f32[16,1024,128]{1,0,2:T(8,128)} %copy.166), calls=%async_computation.7 | async-start | bytes 16777216 | tf_op jit(solution)/shard_map/all_to_all | solution.py:127
  1439.5 12.8 copy-start.7
  1439.5 12.8 copy-start.8
  1452.3 16.7 copy-start
  1452.3 30.5 %slice-start = ((s8[8388608]{0:T(1024)(128)(4,1)}), s8[4194304]{0:T(1024)(128)(4,1)S(1)}, s32[]{:S(2)}) async-start(s8[8388608]{0:T(1024)(128)(4,1)} %bitcast.247), calls=%async_computation.10 | async-start | bytes 8388608
  1469.0 13.8 slice-start.1
  1482.8 12.1 copy-start.10
  1514.2 14.3 copy-start.5
  1585.1 5.0 copy-start.14
  1585.1 97.6 %all-to-all-start.9 = ((f32[8,1,131072]{2,1,0:T(1,128)}), f32[8,1,131072]{2,1,0:T(1,128)}, u32[]{:S(2)}, u32[]{:S(2)}) async-start(f32[8,1,131072]{2,1,0:T(1,128)} %reshape.300), calls=%async_computation.9 | async-start | bytes 8388608 | tf_op jit(solution)/shard_map/all_to_all | solution.py:144
  1590.0 6.7 copy-start.4
  1753.1 44.5 %copy-start.16 = (f32[16]{0:T(128)S(1)}, f32[16]{0:T(128)}, u32[]{:S(2)}) copy-start(f32[16]{0:T(128)} %param.7) | copy-start | bytes 196
where the time goes:
time: 1810 us; the launch traced here: 1800 us
  local copies, waits for them, and re-layouts  746 us (41%)
  waiting for transfers between devices  541 us (30%)
  matrix products  289 us (16%)
  other arithmetic  168 us (9%)
  starting transfers between devices  59.2 us (3%)
    unnamed x57, local copies, waits for them, and re-layouts  313 us
    all_to_all x1, waiting for transfers between devices, body(): lax.all_to_all(imag_part, 'seq', split_axis=2, concat_axis=1, tiled=True)  151 us
    all_to_all x1, waiting for transfers between devices, body(): lax.all_to_all(real_part, 'seq', split_axis=2, concat_axis=1, tiled=True)  144 us
    dot_general x12, matrix products, dft_apply(): second = product(mat_real, imag_part) + product(mat_imag, real_part)  133 us
    dot_general x12, matrix products, dft_apply(): first = product(mat_real, real_part) - product(mat_imag, imag_part)  113 us
    all_to_all x1, waiting for transfers between devices, body(): lax.all_to_all(projected, 'chan', split_axis=1, concat_axis=2, tiled=True)  93 us
    all_to_all x1, waiting for transfers between devices, body(): lax.all_to_all(spatial, 'seq', split_axis=1, concat_axis=2, tiled=True)  81.5 us
    unnamed x4, other arithmetic  77 us
  transfers between devices with their start and end apart: 10, of which 5 were waited for; matrix products, arithmetic and copies ran while one was open for 39% of the time, Pallas kernels for 0%

commit v1 on v0

v1 whole, which is shorter than its diff:
```python
import math

import jax
import jax.numpy as jnp
import numpy as np
from jax import lax
from jax.sharding import PartitionSpec as P

P1 = 128
HALF = 64
Q = 64
R = 128
N = P1 * Q * R


def roots(exponent, total):
    angles = 2.0 * math.pi / total * (np.asarray(exponent, np.int64) % total)
    return np.cos(angles), -np.sin(angles)


def tables():
    k1, n1 = np.arange(P1), np.arange(HALF)
    k2, n3 = np.arange(Q), np.arange(R)
    fr, fi = roots(np.outer(k1, n1), P1)
    first = np.block([[fr, -fi], [fi, fr]])
    last = np.block([[fr.T, fi.T], [-fi.T, fr.T]]) / N
    tr, ti = roots(np.outer(k1, k2), P1 * Q)
    sr, si = roots(np.outer(k2, k2), Q)
    cr, ci = roots(np.outer(n3, n3), R)
    ar, ai = roots(np.outer(k1, n3), N)
    br, bi = roots(np.outer(k2, n3), Q * R)
    return [
        np.asarray(t, np.float32) for t in (first, last, tr, ti, sr, si, cr, ci, ar, ai, br, bi)
    ]


def dot(form, a, b):
    return jnp.einsum(form, a, b, precision=lax.Precision.HIGHEST)


def turn(re, im, c, s):
    return re * c - im * s, re * s + im * c


def forward(first, parts, tabs):
    _, _, tr, ti, sr, si, cr, ci, wr, wi = tabs
    flat = dot("kn,nm->km", first, parts)
    re, im = flat[:P1].reshape(P1, Q, R), flat[P1:].reshape(P1, Q, R)
    re, im = turn(re, im, tr[:, :, None], ti[:, :, None])
    re, im = (
        dot("kn,pnr->pkr", sr, re) - dot("kn,pnr->pkr", si, im),
        dot("kn,pnr->pkr", sr, im) + dot("kn,pnr->pkr", si, re),
    )
    re, im = turn(re, im, wr, wi)
    return (
        dot("pqr,rk->pqk", re, cr) - dot("pqr,rk->pqk", im, ci),
        dot("pqr,rk->pqk", im, cr) + dot("pqr,rk->pqk", re, ci),
    )


def backward(re, im, tabs):
    _, last, tr, ti, sr, si, cr, ci, wr, wi = tabs
    re, im = (
        dot("pqr,rk->pqk", re, cr) + dot("pqr,rk->pqk", im, ci),
        dot("pqr,rk->pqk", im, cr) - dot("pqr,rk->pqk", re, ci),
    )
    re, im = turn(re, im, wr, -wi)
    re, im = (
        dot("kn,pnr->pkr", sr, re) + dot("kn,pnr->pkr", si, im),
        dot("kn,pnr->pkr", sr, im) - dot("kn,pnr->pkr", si, re),
    )
    re, im = turn(re, im, tr[:, :, None], -ti[:, :, None])
    flat = jnp.concatenate([re, im], 0).reshape(2 * P1, Q * R)
    return dot("kn,nm->km", last, flat)


def body(projected, live_blocks, filters, skip_gain):
    seq, chan = lax.axis_size("seq"), lax.axis_size("chan")
    at_seq, at_chan = lax.axis_index("seq"), lax.axis_index("chan")
    channels, here = projected.shape[1], projected.shape[2]
    own = channels // chan
    pairs = own // 2
    copies = seq // pairs
    sub = live_blocks.shape[0] // chan
    span = here * chan
    keep = lax.dynamic_slice_in_dim(live_blocks, at_chan * sub, sub).astype(jnp.float32)
    keep = jnp.broadcast_to(keep[:, None], (sub, R)).reshape(1, here)
    product = (
        projected[1].astype(jnp.float32) * projected[2].astype(jnp.float32) * keep
    ).astype(jnp.bfloat16)
    rows = product.reshape(chan, pairs, 2, here // R, R)
    rows = jnp.repeat(rows, copies, axis=1) if copies > 1 else rows
    rows = rows.transpose(1, 0, 2, 3, 4).reshape(seq * chan, 2, here // R, R)
    rows = lax.all_to_all(rows, ("seq", "chan"), split_axis=0, concat_axis=0, tiled=True)
    taps = lax.all_gather(filters, "seq", axis=1, tiled=True)
    gate = lax.all_to_all(projected[0], "chan", split_axis=0, concat_axis=1, tiled=True)
    first, last, tr, ti, sr, si, cr, ci, ar, ai, br, bi = tables()
    wr, wi = turn(ar[:, None, :], ai[:, None, :], br[None], bi[None])
    tabs = (first, last, tr, ti, sr, si, cr, ci, wr, wi)
    signal = rows.transpose(1, 0, 2, 3).reshape(2 * HALF, Q * R).astype(jnp.float32)
    hr, hi = forward(first[:, :HALF], taps.reshape(HALF, Q * R), tabs)
    re, im = forward(first, signal, tabs)
    re, im = turn(re, im, hr, hi)
    convolved = backward(re, im, tabs)
    pair = at_seq // copies
    gain = lax.dynamic_slice_in_dim(skip_gain, 2 * pair, 2)
    gain = jnp.repeat(gain, HALF)[:, None]
    summed = (convolved + gain * signal).astype(jnp.bfloat16)
    summed = summed.reshape(2, seq, span // R, R).transpose(1, 0, 2, 3)
    summed = lax.all_to_all(summed, "seq", split_axis=0, concat_axis=0, tiled=True)
    summed = summed[::copies].reshape(own, span)
    return (gate.astype(jnp.float32) * summed.astype(jnp.float32)).astype(jnp.bfloat16)


def solution(mesh):
    in_specs = (P(None, None, ("seq", "chan")), P("seq"), P("chan", "seq"), P("chan"))
    out_specs = P("chan", "seq")
    return jax.shard_map(body, mesh=mesh, in_specs=in_specs, out_specs=out_specs, check_vma=False)
```

time: 1810 us -> 405 us (0.22)
  local copies, waits for them, and re-layouts: 746 us -> 38.2 us
  waiting for transfers between devices: 541 us -> 100 us
  other arithmetic: 168 us -> 46.3 us
  matrix products: 289 us -> 184 us
  starting transfers between devices: 59.2 us -> 15.8 us
    all_to_all x10 -> x3, waiting for transfers between devices: 541 us -> 44.8 us  [the longest x1 44.8 us: body(): lax.all_to_all(summed, 'seq', split_axis=0, concat_axis=0, tiled=True)]
    unnamed x57 -> x41, local copies, waits for them, and re-layouts: 313 us -> 20.1 us
    reshape x12 -> x4, local copies, waits for them, and re-layouts: 220 us -> 10.4 us  [the longest x2 4.38 us: body(): summed = summed.reshape(2, seq, span // R, R).transpose(1, 0, 2, 3)]
    all_to_all x12 -> x0, local copies, waits for them, and re-layouts: 159 us -> none  [the longest x1 40.1 us: body(): lax.all_to_all(real_part, 'seq', split_axis=1, concat_axis=2, tiled=True)]
    dot_general x30 -> x27, matrix products: 289 us -> 184 us  [dot(): return jnp.einsum(form, a, b, precision=lax.Precision.HIGHEST)]
    all_to_all x5 -> x0, other arithmetic: 71 us -> none  [the longest x1 26.6 us: body(): lax.all_to_all(real_part, 'seq', split_axis=1, concat_axis=2, tiled=True)]
    unnamed x4 -> x3, other arithmetic: 77 us -> 6.93 us
    all_gather x0 -> x1, waiting for transfers between devices: none -> 54.7 us  [body(): taps = lax.all_gather(filters, 'seq', axis=1, tiled=True)]
  transfers between devices with their start and end apart: 10 -> 4, of which waited for: 5 -> 2; matrix products, arithmetic and copies ran while one was open for 39% -> 66% of each run, Pallas kernels for 0% -> 0%
where the time goes in v1:
time: 405 us; the launch traced here: 399 us
  matrix products  184 us (45%)
  waiting for transfers between devices  100 us (25%)
  other arithmetic  46.3 us (11%)
  local copies, waits for them, and re-layouts  38.2 us (9%)
  starting transfers between devices  15.8 us (4%)
  between operations  14 us (3%)
    dot_general x27, matrix products, dot(): return jnp.einsum(form, a, b, precision=lax.Precision.HIGHEST)  184 us
    all_gather x1, waiting for transfers between devices, body(): taps = lax.all_gather(filters, 'seq', axis=1, tiled=True)  54.7 us
    all_to_all x1, waiting for transfers between devices, body(): lax.all_to_all(summed, 'seq', split_axis=0, concat_axis=0, tiled=True)  44.8 us
    unnamed x41, local copies, waits for them, and re-layouts  20.1 us
    all_gather x1, other arithmetic, body(): taps = lax.all_gather(filters, 'seq', axis=1, tiled=True)  18.4 us
  transfers between devices with their start and end apart: 4, of which 2 were waited for; matrix products, arithmetic and copies ran while one was open for 66% of the time, Pallas kernels for 0%

profile of v1, /device:TPU:0, one launch (start us, length us, event | category | flops | bytes accessed | tf_op | source)
XLA Modules:
  0.0 398.9 jit_solution(1892564629985002507)
XLA Ops:
  7.3 4.7 %multiply_bitcast_fusion = f32[8,8,128,128]{3,1,2,0:T(8,128)} fusion(bf16[3,64,16384]{2,1,0:T(8,128)(2,1)} %param.40), kind=kLoop, calls=%fused_computation.36 | loop fusion | flops 3145728 | bytes 8388608
  11.9 4.9 %copy.88 = f32[8,8,128,128]{3,2,1,0:T(8,128)} copy(f32[8,8,128,128]{3,1,2,0:T(8,128)} %multiply_bitcast_fusion) | data formatting | bytes 8388608
  17.6 4.3 %fusion.8 = bf16[4,8,2,128,128]{4,3,2,0,1:T(8,128)(2,1)} fusion(f32[4,8,2,128,128]{4,3,2,1,0:T(8,128)} %bitcast.127, f32[128]{0:T(128)S(1)} %dynamic-slice_convert_fusion), kind=kLoop, calls=%fused_computation.24 | loop fusion | flops 2097152 | bytes 6291968 | tf_op jit(solution)/shard_map/convert_element_type | solution.py:90
  21.8 7.4 %all-to-all-start.1 = ((bf16[32,2,128,128]{3,2,1,0:T(8,128)(2,1)}), bf16[32,2,128,128]{3,2,1,0:T(8,128)(2,1)S(1)}, u32[]{:S(2)}, u32[]{:S(2)}) async-start(bf16[32,2,128,128]{3,2,1,0:T(8,128)(2,1)} %bitcast.3), calls=%async_computation.1 | async-start | bytes 4194304 | tf_op jit(solution)/shard_map/all_to_all | solution.py:94
  32.5 54.7 %all-gather.2.cloned.1.call-done = f32[1,524288]{1,0:T(1,128)} async-done(((f32[1,65536]{1,0:T(1,128)}), f32[1,524288]{1,0:T(1,128)}) %all-gather.2.cloned.1.call-update) | async-done | bytes 2097168 | tf_op jit(solution)/shard_map/all_gather | solution.py:95
  87.8 18.4 %reduce.3 = f32[524288]{0:T(1024)} reduce(f32[1,524288]{1,0:T(1,128)} %all-gather.2.cloned.1.call-done, f32[]{:T(128)} %broadcast.15), dimensions={0}, to_apply=%all_gather.3.reduce_sub_computation.3 | reduce | bytes 4194308 | tf_op jit(solution)/shard_map/all_gather | solution.py:95
  109.3 8.4 %fusion.56 = f32[256,8192]{1,0:T(8,128)S(1)} fusion(f32[256,64]{1,0:T(8,128)S(1)} %copy-done.13, f32[64,8192]{1,0:T(8,128)} %reshape.55), kind=kOutput, calls=%fused_computation.79 | convolution fusion | flops 1610612736 | bytes 10551296 | tf_op jit(solution)/shard_map/kn,nm->km/dot_general | solution.py:38
  124.1 4.7 %all-to-all-start = ((bf16[4,16,16384]{2,1,0:T(8,128)(2,1)}), bf16[4,16,16384]{2,1,0:T(8,128)(2,1)}, u32[]{:S(2)}, u32[]{:S(2)}) async-start(bf16[4,16,16384]{2,1,0:T(8,128)(2,1)} %bitcast), calls=%async_computation | async-start | bytes 4194304 | tf_op jit(solution)/shard_map/all_to_all | solution.py:96
  143.8 7.9 %fusion.4 = (f32[128,64,128]{2,1,0:T(8,128)S(1)}, f32[128,64,128]{2,1,0:T(8,128)S(1)}, f32[128,64,128]{2,1,0:T(8,128)S(1)}, f32[128,64,128]{2,1,0:T(8,128)S(1)}) fusion(f32[16,8,64,128]{3,2,1,0:T(8,128)} %copy.92, f32[16,8,64,128]{3,2,1,0:T(8,128)S(1)} %copy-done.5, f32[128,64]{1,0:T(8,128)S(1)} %copy-done.15, f32[128,64]{1,0:T(8,128)S(1)} %copy-done.10, ...), kind=kLoop, calls=%fused_computation.9 | loop fusion | flops 12582912 | bytes 33619968 | tf_op jit(solution)/shard_map/sub | solution.py:42
  151.8 4.2 %fusion.55 = f32[128,128,64]{1,2,0:T(8,128)S(1)} fusion(f32[128,64,128]{2,1,0:T(8,128)S(1)} %get-tuple-element.25, f32[64,64,1]{1,0,2:T(8,128)S(1)} %copy-done.9), kind=kOutput, calls=%fused_computation.78 | convolution fusion | flops 805306368 | bytes 8404992 | tf_op jit(solution)/shard_map/kn,pnr->pkr/dot_general | solution.py:38
  159.9 4.0 fusion.58
  163.9 5.8 %fusion.54 = f32[128,128,64]{1,2,0:T(8,128)} fusion(f32[128,64,128]{2,1,0:T(8,128)S(1)} %get-tuple-element.26, f32[64,64,1]{1,0,2:T(8,128)S(1)} %copy-done.9), kind=kOutput, calls=%fused_computation.77 | convolution fusion | flops 805306368 | bytes 8404992 | tf_op jit(solution)/shard_map/kn,pnr->pkr/dot_general | solution.py:38
  169.7 5.6 %convolution_add_fusion.3 = f32[128,128,64]{1,2,0:T(8,128)} fusion(f32[128,128,64]{1,2,0:T(8,128)S(1)} %fusion.55, f32[128,64,128]{2,1,0:T(8,128)S(1)} %get-tuple-element.26, f32[64,64,1]{1,0,2:T(8,128)S(1)} %copy-done.8), kind=kOutput, calls=%fused_computation.71 | convolution fusion | flops 806354944 | bytes 12599296 | tf_op jit(solution)/shard_map/kn,pnr->pkr/dot_general | solution.py:38
  175.3 5.4 %convolution_subtract_fusion.1 = f32[128,128,64]{1,2,0:T(8,128)} fusion(f32[128,128,64]{1,2,0:T(8,128)S(1)} %fusion.57, f32[128,64,128]{2,1,0:T(8,128)S(1)} %get-tuple-element.16, f32[64,64,1]{1,0,2:T(8,128)S(1)} %copy-done.8), kind=kOutput, calls=%fused_computation.70 | convolution fusion | flops 806354944 | bytes 12599296 | tf_op jit(solution)/shard_map/kn,pnr->pkr/dot_general | solution.py:38
  180.6 5.3 %convolution_add_fusion.2 = f32[128,128,64]{1,2,0:T(8,128)} fusion(f32[128,128,64]{1,2,0:T(8,128)S(1)} %fusion.58, f32[128,64,128]{2,1,0:T(8,128)S(1)} %get-tuple-element.15, f32[64,64,1]{1,0,2:T(8,128)S(1)} %copy-done.8), kind=kOutput, calls=%fused_computation.69 | convolution fusion | flops 806354944 | bytes 12599296 | tf_op jit(solution)/shard_map/kn,pnr->pkr/dot_general | solution.py:38
  186.0 15.6 %subtract_bitcast_fusion = (f32[128,64,128]{2,1,0:T(8,128)}, f32[128,64,128]{2,1,0:T(8,128)}, f32[128,64,128]{2,1,0:T(8,128)}, f32[128,64,128]{2,1,0:T(8,128)S(1)}) fusion(f32[128,128,64]{1,2,0:T(8,128)} %convolution_add_fusion.2, f32[128,128,64]{1,2,0:T(8,128)} %constant.74, f32[128,128,64]{1,2,0:T(8,128)} %convolution_subtract_fusion.1, ...), kind=kOutput, calls=%fused_computation.27 | convolution fusion | flops 818937856 | bytes 46153728 | tf_op jit(solution)/shard_map/kn,pnr->pkr/dot_general | solution.py:38
  201.6 8.3 %fusion.19 = f32[128,64,128]{2,0,1:T(8,128)S(1)} fusion(f32[128,128,1]{1,0,2:T(8,128)S(1)} %copy-done.6, f32[128,64,128]{2,1,0:T(8,128)} %get-tuple-element.10), kind=kOutput, calls=%fused_computation.47 | convolution fusion | flops 1610612736 | bytes 8454144 | tf_op jit(solution)/shard_map/pqr,rk->pqk/dot_general | solution.py:38
  210.0 6.9 %fusion.27 = f32[128,64,128]{2,0,1:T(8,128)S(1)} fusion(f32[128,128,1]{1,0,2:T(8,128)S(1)} %copy-done.6, f32[128,64,128]{2,1,0:T(8,128)S(1)} %copy-done.1), kind=kOutput, calls=%fused_computation.55 | convolution fusion | flops 1610612736 | bytes 8454144 | tf_op jit(solution)/shard_map/pqr,rk->pqk/dot_general | solution.py:38
  216.9 7.3 %fusion.17 = f32[128,64,128]{2,0,1:T(8,128)S(1)} fusion(f32[128,128,1]{1,0,2:T(8,128)S(1)} %copy-done.7, f32[128,64,128]{2,1,0:T(8,128)S(1)} %copy-done.2), kind=kOutput, calls=%fused_computation.45 | convolution fusion | flops 1610612736 | bytes 8454144 | tf_op jit(solution)/shard_map/pqr,rk->pqk/dot_general | solution.py:38
  224.2 7.8 %fusion.25 = f32[128,64,128]{2,0,1:T(8,128)} fusion(f32[128,128,1]{1,0,2:T(8,128)S(1)} %copy-done.7, f32[128,64,128]{2,1,0:T(8,128)S(1)} %copy-done.1), kind=kOutput, calls=%fused_computation.53 | convolution fusion | flops 1610612736 | bytes 8454144 | tf_op jit(solution)/shard_map/pqr,rk->pqk/dot_general | solution.py:38
  232.0 6.6 %fusion.39 = f32[128,64,128]{2,0,1:T(8,128)S(1)} fusion(f32[128,64,128]{2,0,1:T(8,128)S(1)} %fusion.19, f32[128,128,1]{1,0,2:T(8,128)S(1)} %copy-done.7, f32[128,64,128]{2,1,0:T(8,128)S(1)} %copy-done), kind=kOutput, calls=%fused_computation.63 | convolution fusion | flops 1611661312 | bytes 12648448 | tf_op jit(solution)/shard_map/pqr,rk->pqk/dot_general | solution.py:38
  238.6 6.8 %fusion.42 = f32[128,64,128]{2,0,1:T(8,128)S(1)} fusion(f32[128,64,128]{2,0,1:T(8,128)S(1)} %fusion.17, f32[128,128,1]{1,0,2:T(8,128)S(1)} %copy-done.6, f32[128,64,128]{2,1,0:T(8,128)S(1)} %copy-done), kind=kOutput, calls=%fused_computation.64 | convolution fusion | flops 1611661312 | bytes 12648448 | tf_op jit(solution)/shard_map/pqr,rk->pqk/dot_general | solution.py:38
  245.4 8.1 %fusion.33 = f32[128,64,128]{2,0,1:T(8,128)} fusion(f32[128,64,128]{2,0,1:T(8,128)S(1)} %fusion.27, f32[128,128,1]{1,0,2:T(8,128)S(1)} %copy-done.7, f32[128,64,128]{2,1,0:T(8,128)S(1)} %get-tuple-element.20), kind=kOutput, calls=%fused_computation.61 | convolution fusion | flops 1611661312 | bytes 12648448 | tf_op jit(solution)/shard_map/pqr,rk->pqk/dot_general | solution.py:38
  253.5 9.4 %multiply_subtract_fusion.1 = (f32[128,64,128]{2,0,1:T(8,128)S(1)}, f32[128,64,128]{2,0,1:T(8,128)S(1)}) fusion(f32[128,64,128]{2,0,1:T(8,128)S(1)} %fusion.42, f32[128,64,128]{2,0,1:T(8,128)} %fusion.33, f32[128,64,128]{2,0,1:T(8,128)S(1)} %fusion.39, f32[128,64,128]{2,0,1:T(8,128)} %fusion.25, f32[128,128,1]{1,0,2:T(8,128)S(1)} %copy-done.6, ...), kind=kOutput, calls=%fused_computation.35 | convolution fusion | flops 1617952768 | bytes 29425664 | tf_op jit(solution)/shard_map/pqr,rk->pqk/dot_general | solution.py:38
  273.1 6.8 %multiply_subtract_fusion = (f32[128,64,128]{2,0,1:T(8,128)S(1)}, f32[128,64,128]{2,0,1:T(8,128)S(1)}) fusion(f32[128,64,128]{2,0,1:T(8,128)} %constant.66.clone, f32[128,64,128]{2,0,1:T(8,128)S(1)} %convolution_add_fusion.1, f32[128,64,128]{2,0,1:T(8,128)} %constant.61.clone, f32[128,64,128]{2,0,1:T(8,128)S(1)} %fusion.60, ...), kind=kOutput, calls=%fused_computation.33 | convolution fusion | flops 1617952768 | bytes 29425664 | tf_op jit(solution)/shard_map/pqr,rk->pqk/dot_general | solution.py:38
  280.0 6.4 %fusion.11 = f32[128,128,64]{1,2,0:T(8,128)S(1)} fusion(f32[64,64,1]{1,0,2:T(8,128)S(1)} %copy-done.8, f32[128,64,128]{2,0,1:T(8,128)S(1)} %get-tuple-element.6), kind=kOutput, calls=%fused_computation.39 | convolution fusion | flops 805306368 | bytes 8404992 | tf_op jit(solution)/shard_map/kn,pnr->pkr/dot_general | solution.py:38
  286.4 6.6 %fusion.9 = f32[128,128,64]{1,2,0:T(8,128)S(1)} fusion(f32[64,64,1]{1,0,2:T(8,128)S(1)} %copy-done.9, f32[128,64,128]{2,0,1:T(8,128)S(1)} %get-tuple-element.6), kind=kOutput, calls=%fused_computation.37 | convolution fusion | flops 805306368 | bytes 8404992 | tf_op jit(solution)/shard_map/kn,pnr->pkr/dot_general | solution.py:38
  293.0 6.4 %fusion.45 = f32[128,128,64]{1,2,0:T(8,128)S(1)} fusion(f32[128,128,64]{1,2,0:T(8,128)S(1)} %fusion.11, f32[64,64,1]{1,0,2:T(8,128)S(1)} %copy-done.9, f32[128,64,128]{2,0,1:T(8,128)S(1)} %get-tuple-element.5), kind=kOutput, calls=%fused_computation.65 | convolution fusion | flops 806354944 | bytes 12599296 | tf_op jit(solution)/shard_map/kn,pnr->pkr/dot_general | solution.py:38
  299.4 11.0 %subtract_bitcast_fusion.2 = (f32[128,64,128]{2,1,0:T(8,128)}, f32[128,64,128]{2,1,0:T(8,128)}) fusion(f32[128,128,64]{1,2,0:T(8,128)S(1)} %fusion.45, f32[128,64]{1,0:T(8,128)S(1)} %copy-done.14, f32[128,64]{1,0:T(8,128)S(1)} %copy-done.10, f32[128,128,64]{1,2,0:T(8,128)S(1)} %fusion.9, f32[64,64,1]{1,0,2:T(8,128)S(1)} %copy-done.8, ...), kind=kOutput, calls=%fused_computation.31 | convolution fusion | flops 812646400 | bytes 21053440 | tf_op jit(solution)/shard_map/kn,pnr->pkr/dot_general | solution.py:38
  310.4 4.3 %pad_maximum_fusion = f32[256,64,128]{2,1,0:T(8,128)S(1)} fusion(f32[128,64,128]{2,1,0:T(8,128)} %get-tuple-element.14, f32[128,64,128]{2,1,0:T(8,128)} %get-tuple-element.13), kind=kLoop, calls=%fused_computation.4 | loop fusion | flops 2097152 | bytes 16777216 | tf_op jit(solution)/shard_map/concatenate | solution.py:73
  314.7 14.1 %fusion = bf16[128,8192]{1,0:T(8,128)(2,1)} fusion(f32[128,256]{1,0:T(8,128)S(1)} %copy-done.11, f32[32,8,64,128]{3,2,1,0:T(8,128)S(1)} %bitcast.125, bf16[128,8192]{1,0:T(8,128)(2,1)S(1)} %reshape.52, f32[128]{0:T(128)S(1)} %mul.225), kind=kOutput, calls=%fused_computation.1 | convolution fusion | flops 3225419776 | bytes 12714496 | tf_op jit(solution)/shard_map/kn,nm->km/dot_general | solution.py:38
  341.1 44.8 %all-to-all-done.2 = bf16[8,2,512,128]{3,2,1,0:T(8,128)(2,1)S(1)} async-done(((bf16[8,2,512,128]{3,2,1,0:T(8,128)(2,1)}), bf16[8,2,512,128]{3,2,1,0:T(8,128)(2,1)S(1)}, u32[]{:S(2)}, u32[]{:S(2)}) %all-to-all-start.2) | async-done | bytes 2097184 | tf_op jit(solution)/shard_map/all_to_all | solution.py:110
  (65 shorter events, 62.3 us)
Async XLA Ops:
  6.5 80.6 %all-gather.2.cloned.1.call-start = ((), (), s32[]{:S(2)}) async-start(), calls=%async_computation.3 | async-start | bytes 2359296 | tf_op jit(solution)/shard_map/all_gather | solution.py:95
  21.8 10.4 %copy-start.16 = (f32[16]{0:T(128)S(1)}, f32[16]{0:T(128)}, u32[]{:S(2)}) copy-start(f32[16]{0:T(128)} %param.43) | copy-start | bytes 196
  21.8 102.3 %all-to-all-start.1 = ((bf16[32,2,128,128]{3,2,1,0:T(8,128)(2,1)}), bf16[32,2,128,128]{3,2,1,0:T(8,128)(2,1)S(1)}, u32[]{:S(2)}, u32[]{:S(2)}) async-start(bf16[32,2,128,128]{3,2,1,0:T(8,128)(2,1)} %bitcast.3), calls=%async_computation.1 | async-start | bytes 4194304 | tf_op jit(solution)/shard_map/all_to_all | solution.py:94
  87.7 21.6 %copy-start.13 = (f32[256,64]{1,0:T(8,128)S(1)}, f32[256,64]{1,0:T(8,128)}, u32[]{:S(2)}) copy-start(f32[256,64]{1,0:T(8,128)} %constant.56.clone) | copy-start | bytes 196612
  124.1 209.1 %all-to-all-start = ((bf16[4,16,16384]{2,1,0:T(8,128)(2,1)}), bf16[4,16,16384]{2,1,0:T(8,128)(2,1)}, u32[]{:S(2)}, u32[]{:S(2)}) async-start(bf16[4,16,16384]{2,1,0:T(8,128)(2,1)} %bitcast), calls=%async_computation | async-start | bytes 4194304 | tf_op jit(solution)/shard_map/all_to_all | solution.py:96
  128.8 4.4 %copy-start.12 = (f32[256,128]{1,0:T(8,128)S(1)}, f32[256,128]{1,0:T(8,128)}, u32[]{:S(2)}) copy-start(f32[256,128]{1,0:T(8,128)} %constant.65.clone) | copy-start | bytes 393220
  140.3 3.4 copy-start.5
  140.3 3.4 copy-start.10
  140.3 3.5 copy-start.15
  143.8 8.0 %copy-start.9 = (f32[64,64,1]{1,0,2:T(8,128)S(1)}, f32[64,64,1]{1,0,2:T(8,128)}, u32[]{:S(2)}) copy-start(f32[64,64,1]{1,0,2:T(8,128)} %constant.81) | copy-start | bytes 49156
  151.7 4.2 %copy-start.3 = (f32[128,64,128]{2,1,0:T(8,128)}, f32[128,64,128]{2,1,0:T(8,128)S(1)}, u32[]{:S(2)}) copy-start(f32[128,64,128]{2,1,0:T(8,128)S(1)} %get-tuple-element.25) | copy-start | bytes 12582916
  163.9 5.8 %copy-start.8 = (f32[64,64,1]{1,0,2:T(8,128)S(1)}, f32[64,64,1]{1,0,2:T(8,128)}, u32[]{:S(2)}) copy-start(f32[64,64,1]{1,0,2:T(8,128)} %constant.82) | copy-start | bytes 49156
  186.0 15.6 %copy-start.6 = (f32[128,128,1]{1,0,2:T(8,128)S(1)}, f32[128,128,1]{1,0,2:T(8,128)}, u32[]{:S(2)}) copy-start(f32[128,128,1]{1,0,2:T(8,128)} %constant.84) | copy-start | bytes 196612
  201.6 8.3 %copy-start.1 = (f32[128,64,128]{2,1,0:T(8,128)S(1)}, f32[128,64,128]{2,1,0:T(8,128)}, u32[]{:S(2)}) copy-start(f32[128,64,128]{2,1,0:T(8,128)} %get-tuple-element.19) | copy-start | bytes 12582916
  209.9 6.9 %copy-start.2 = (f32[128,64,128]{2,1,0:T(8,128)S(1)}, f32[128,64,128]{2,1,0:T(8,128)}, u32[]{:S(2)}) copy-start(f32[128,64,128]{2,1,0:T(8,128)} %get-tuple-element.10) | copy-start | bytes 12582916
  209.9 6.9 %copy-start.7 = (f32[128,128,1]{1,0,2:T(8,128)S(1)}, f32[128,128,1]{1,0,2:T(8,128)}, u32[]{:S(2)}) copy-start(f32[128,128,1]{1,0,2:T(8,128)} %constant.83) | copy-start | bytes 196612
  224.2 7.8 %copy-start = (f32[128,64,128]{2,1,0:T(8,128)S(1)}, f32[128,64,128]{2,1,0:T(8,128)}, u32[]{:S(2)}) copy-start(f32[128,64,128]{2,1,0:T(8,128)} %get-tuple-element.9) | copy-start | bytes 12582916
  293.0 6.4 %copy-start.14 = (f32[128,64]{1,0:T(8,128)S(1)}, f32[128,64]{1,0:T(8,128)}, u32[]{:S(2)}) copy-start(f32[128,64]{1,0:T(8,128)} %constant.72) | copy-start | bytes 98308
  310.4 4.3 %copy-start.11 = (f32[128,256]{1,0:T(8,128)S(1)}, f32[128,256]{1,0:T(8,128)}, u32[]{:S(2)}) copy-start(f32[128,256]{1,0:T(8,128)} %constant.68.clone) | copy-start | bytes 393220
  333.2 52.7 %all-to-all-start.2 = ((bf16[8,2,512,128]{3,2,1,0:T(8,128)(2,1)}), bf16[8,2,512,128]{3,2,1,0:T(8,128)(2,1)S(1)}, u32[]{:S(2)}, u32[]{:S(2)}) async-start(bf16[8,2,512,128]{3,2,1,0:T(8,128)(2,1)} %bitcast.130), calls=%async_computation.2 | async-start | bytes 4194304 | tf_op jit(solution)/shard_map/all_to_all | solution.py:110
  385.9 2.2 copy-start.4
Sparse Core Ops, SparseCore 0:
  9.5 77.6 all-gather.1

commit v2 on v1

v2 whole, which is shorter than its diff:
```python
import math

import jax
import jax.numpy as jnp
import numpy as np
from jax import lax
from jax.experimental import pallas as pl
from jax.experimental.pallas import tpu as pltpu
from jax.sharding import PartitionSpec as P

P1 = 128
HALF = 64
Q = 64
R = 128
N = P1 * Q * R


def roots(exponent, total):
    angles = 2.0 * math.pi / total * (np.asarray(exponent, np.int64) % total)
    return np.cos(angles), -np.sin(angles)


def halves(matrix):
    high = np.asarray(matrix, np.float32).astype(jnp.bfloat16)
    low = (np.asarray(matrix) - high.astype(np.float64)).astype(jnp.bfloat16)
    return high, low


def thrice(matrix, axis):
    high, low = halves(matrix)
    return np.concatenate([high, high, low], axis)


def tables():
    k1, n1 = np.arange(P1), np.arange(HALF)
    k2, n3 = np.arange(Q), np.arange(R)
    fr, fi = roots(np.outer(k1, n1), P1)
    sr, si = roots(np.outer(k2, k2), Q)
    cr, ci = roots(np.outer(n3, n3), R)
    ar, ai = roots(np.outer(k1, n3), N)
    gr, gi = roots(np.outer(k1, np.ones(R, np.int64)), P1 * Q)
    br, bi = roots(np.outer(k2, n3), Q * R)
    return {
        "first": np.concatenate(halves(np.block([[fr, -fi], [fi, fr]])), 1),
        "taps": thrice(np.concatenate([fr, fi], 0), 1),
        "last": thrice(np.block([[fr.T, fi.T], [-fi.T, fr.T]]) / N, 1),
        "second": thrice(np.concatenate([sr, si], 0), 1),
        "second_back": thrice(np.concatenate([sr, -si], 0), 1),
        "third": thrice(np.block([[cr, ci], [-ci, cr]]), 0),
        "third_back": thrice(np.block([[cr, -ci], [ci, cr]]), 0),
        "start": np.stack([ar, ai]).astype(np.float32),
        "step": np.stack([gr, gi]).astype(np.float32),
        "outer": np.stack([br, bi]).astype(np.float32),
    }


def turn(re, im, c, s):
    return re * c - im * s, re * s + im * c


def split(x, axis):
    high = x.astype(jnp.bfloat16)
    low = (x - high.astype(jnp.float32)).astype(jnp.bfloat16)
    return jnp.concatenate([high, low, high], axis)


def dot(a, b):
    return jnp.dot(a, b, preferred_element_type=jnp.float32)


WIDE = 4
ROWS = 4


def columns(step):
    return pl.ds(pl.multiple_of(step * WIDE * R, WIDE * R), WIDE * R)


def first_section(load, mat_ref, start_ref, step_ref, out_ref):
    def one(step, carry):
        wr, wi = carry
        flat = dot(mat_ref[...], load(step))
        for part in range(WIDE):
            piece = flat[:, part * R : (part + 1) * R]
            re, im = turn(piece[:P1], piece[P1:], wr, wi)
            where = pl.ds(step * WIDE + part, P1, stride=Q)
            out_ref[0, where, :] = re
            out_ref[1, where, :] = im
            wr, wi = turn(wr, wi, step_ref[0], step_ref[1])
        return wr, wi

    lax.fori_loop(0, Q // WIDE, one, (start_ref[0], start_ref[1]))


def middle(mat_ref, pieces):
    data = jnp.concatenate([x for piece in pieces for x in piece], 1)
    flat = dot(mat_ref[...], split(data, 0))
    done = []
    for part in range(len(pieces)):
        low = flat[:, 2 * part * R : (2 * part + 1) * R]
        high = flat[:, (2 * part + 1) * R : (2 * part + 2) * R]
        done.append((low[:Q] - high[Q:], high[:Q] + low[Q:]))
    return done


def lanes(pieces):
    return jnp.concatenate([jnp.concatenate(piece, 1) for piece in pieces], 0)


def later_sections(src_ref, step, second_ref, third_ref, outer_ref):
    pieces = []
    for part in range(ROWS):
        where = pl.ds(pl.multiple_of((step * ROWS + part) * Q, Q), Q)
        pieces.append((src_ref[0, where, :], src_ref[1, where, :]))
    pieces = middle(second_ref, pieces)
    pieces = [turn(re, im, outer_ref[0], outer_ref[1]) for re, im in pieces]
    return dot(split(lanes(pieces), 1), third_ref[...])


def block(step):
    return pl.ds(pl.multiple_of(step * ROWS * Q, ROWS * Q), ROWS * Q)


def taps_kernel(
    taps_ref, mat_ref, start_ref, step_ref, second_ref, third_ref, outer_ref, out_ref, held
):
    def load(step):
        return split(taps_ref[:, columns(step)], 0)

    first_section(load, mat_ref, start_ref, step_ref, held)

    def one(step, carry):
        flat = later_sections(held, step, second_ref, third_ref, outer_ref)
        out_ref[0, block(step), :] = flat[:, :R]
        out_ref[1, block(step), :] = flat[:, R:]
        return carry

    lax.fori_loop(0, P1 // ROWS, one, 0)


def signal_kernel(
    signal_ref,
    spectrum_ref,
    gain_ref,
    mat_ref,
    last_ref,
    start_ref,
    step_ref,
    second_ref,
    back_ref,
    third_ref,
    third_back_ref,
    outer_ref,
    out_ref,
    held,
):
    def load(step):
        part = signal_ref[:, columns(step)]
        return jnp.concatenate([part, part], 0)

    first_section(load, mat_ref, start_ref, step_ref, held)

    def one(step, carry):
        flat = later_sections(held, step, second_ref, third_ref, outer_ref)
        re, im = turn(
            flat[:, :R], flat[:, R:], spectrum_ref[0, block(step), :], spectrum_ref[1, block(step), :]
        )
        flat = dot(split(jnp.concatenate([re, im], 1), 1), third_back_ref[...])
        pieces = []
        for part in range(ROWS):
            piece = flat[part * Q : (part + 1) * Q]
            pieces.append(turn(piece[:, :R], piece[:, R:], outer_ref[0], -outer_ref[1]))
        pieces = middle(back_ref, pieces)
        for part in range(ROWS):
            where = pl.ds(pl.multiple_of((step * ROWS + part) * Q, Q), Q)
            held[0, where, :] = pieces[part][0]
            held[1, where, :] = pieces[part][1]
        return carry

    lax.fori_loop(0, P1 // ROWS, one, 0)

    def finish(step, carry):
        wr, wi = carry
        found = []
        for part in range(WIDE):
            where = pl.ds(step * WIDE + part, P1, stride=Q)
            re, im = turn(held[0, where, :], held[1, where, :], wr, -wi)
            found.append(jnp.concatenate([re, im], 0))
            wr, wi = turn(wr, wi, step_ref[0], step_ref[1])
        flat = dot(last_ref[...], split(jnp.concatenate(found, 1), 0))
        direct = gain_ref[...] * signal_ref[:, columns(step)].astype(jnp.float32)
        out_ref[:, columns(step)] = (flat + direct).astype(jnp.bfloat16)
        return wr, wi

    lax.fori_loop(0, Q // WIDE, finish, (start_ref[0], start_ref[1]))


def run(kernel, out_shape, out_dtype, flops, *operands):
    return pl.pallas_call(
        kernel,
        out_shape=jax.ShapeDtypeStruct(out_shape, out_dtype),
        in_specs=[pl.BlockSpec(memory_space=pltpu.VMEM)] * len(operands),
        out_specs=pl.BlockSpec(memory_space=pltpu.VMEM),
        scratch_shapes=[pltpu.VMEM((2, P1 * Q, R), jnp.float32)],
        compiler_params=pltpu.CompilerParams(vmem_limit_bytes=52 * 1024 * 1024),
        cost_estimate=pl.CostEstimate(
            flops=flops, bytes_accessed=16 * 1024 * 1024, transcendentals=0
        ),
    )(*operands)


def transform_taps(taps, tabs):
    names = ("taps", "start", "step", "second", "third", "outer")
    return run(
        taps_kernel, (2, P1 * Q, R), jnp.float32, 10**10, taps, *[tabs[name] for name in names]
    )


def convolve(signal, spectrum, gain, tabs):
    names = (
        "first",
        "last",
        "start",
        "step",
        "second",
        "second_back",
        "third",
        "third_back",
        "outer",
    )
    operands = [tabs[name] for name in names]
    return run(
        signal_kernel,
        (2 * HALF, Q * R),
        jnp.bfloat16,
        2 * 10**10,
        signal,
        spectrum,
        gain,
        *operands,
    )


def body(projected, live_blocks, filters, skip_gain):
    seq, chan = lax.axis_size("seq"), lax.axis_size("chan")
    at_seq, at_chan = lax.axis_index("seq"), lax.axis_index("chan")
    channels, here = projected.shape[1], projected.shape[2]
    own = channels // chan
    pairs = own // 2
    copies = seq // pairs
    sub = live_blocks.shape[0] // chan
    span = here * chan
    keep = lax.dynamic_slice_in_dim(live_blocks, at_chan * sub, sub).astype(jnp.float32)
    keep = jnp.broadcast_to(keep[:, None], (sub, R)).reshape(1, here)
    product = (
        projected[1].astype(jnp.float32) * projected[2].astype(jnp.float32) * keep
    ).astype(jnp.bfloat16)
    rows = product.reshape(chan, pairs, 2, here // R, R)
    rows = jnp.repeat(rows, copies, axis=1) if copies > 1 else rows
    rows = rows.transpose(1, 0, 2, 3, 4).reshape(seq * chan, 2, here // R, R)
    rows = lax.all_to_all(rows, ("seq", "chan"), split_axis=0, concat_axis=0, tiled=True)
    taps = lax.all_gather(filters, "seq", axis=1, tiled=True)
    gate = lax.all_to_all(projected[0], "chan", split_axis=0, concat_axis=1, tiled=True)
    tabs = {name: jnp.asarray(table) for name, table in tables().items()}
    signal = rows.transpose(1, 0, 2, 3).reshape(2 * HALF, Q * R)
    spectrum = transform_taps(taps.reshape(HALF, Q * R), tabs)
    pair = at_seq // copies
    gain = lax.dynamic_slice_in_dim(skip_gain, 2 * pair, 2)
    gain = jnp.repeat(gain, HALF)[:, None]
    summed = convolve(signal, spectrum, gain, tabs)
    summed = summed.reshape(2, seq, span // R, R).transpose(1, 0, 2, 3)
    summed = lax.all_to_all(summed, "seq", split_axis=0, concat_axis=0, tiled=True)
    summed = summed[::copies].reshape(own, span)
    return (gate.astype(jnp.float32) * summed.astype(jnp.float32)).astype(jnp.bfloat16)


def solution(mesh):
    in_specs = (P(None, None, ("seq", "chan")), P("seq"), P("chan", "seq"), P("chan"))
    out_specs = P("chan", "seq")
    return jax.shard_map(body, mesh=mesh, in_specs=in_specs, out_specs=out_specs, check_vma=False)
```

time: 405 us -> 280 us (0.69); the launches traced: 399 us -> 279 us
  matrix products: 184 us -> 0 us
  Pallas kernels: 0 us -> 88.2 us
  other arithmetic: 46.3 us -> 34 us
  local copies, waits for them, and re-layouts: 38.2 us -> 27.4 us
    dot_general x27 -> x0, matrix products: 184 us -> none  [dot(): return jnp.einsum(form, a, b, precision=lax.Precision.HIGHEST)]
    pallas_call x0 -> x2, Pallas kernels: none -> 88.2 us  [run(): pl.pallas_call(kernel, out_shape=jax.ShapeDtypeStruct(out_shape, out_dtyp...]
    unnamed x41 -> x27, local copies, waits for them, and re-layouts: 20.1 us -> 6.72 us
    sub x1 -> x0, other arithmetic: 7.94 us -> none  [turn(): return (re * c - im * s, re * s + im * c)]
    concatenate x1 -> x0, other arithmetic: 4.34 us -> none  [backward(): flat = jnp.concatenate([re, im], 0).reshape(2 * P1, Q * R)]
  transfers between devices with their start and end apart: 4 -> 4, of which waited for: 2 -> 2; matrix products, arithmetic and copies ran while one was open for 66% -> 20% of each run, Pallas kernels for 0% -> 32%
where the time goes in v2:
time: 280 us; the launch traced here: 279 us
  waiting for transfers between devices  100 us (36%)
  Pallas kernels  88.2 us (32%)
  other arithmetic  34 us (12%)
  local copies, waits for them, and re-layouts  27.4 us (10%)
  starting transfers between devices  15.6 us (6%)
  between operations  13.6 us (5%)
    pallas_call x2, Pallas kernels, run(): pl.pallas_call(kernel, out_shape=jax.ShapeDtypeStruct(out_shape, out_dtyp...  88.2 us
    all_gather x1, waiting for transfers between devices, body(): taps = lax.all_gather(filters, 'seq', axis=1, tiled=True)  54.6 us
    all_to_all x1, waiting for transfers between devices, body(): lax.all_to_all(summed, 'seq', split_axis=0, concat_axis=0, tiled=True)  44.7 us
    all_gather x1, other arithmetic, body(): taps = lax.all_gather(filters, 'seq', axis=1, tiled=True)  18.4 us
    all_to_all x1, starting transfers between devices, body(): lax.all_to_all(rows, ('seq', 'chan'), split_axis=0, concat_axis=0, tiled=...  7.36 us
    unnamed x3, other arithmetic  6.9 us
    unnamed x27, local copies, waits for them, and re-layouts  6.72 us
  transfers between devices with their start and end apart: 4, of which 2 were waited for; matrix products, arithmetic and copies ran while one was open for 20% of the time, Pallas kernels for 32%

profile of v2, /device:TPU:0, one launch (start us, length us, event | category | flops | bytes accessed | tf_op | source)
XLA Modules:
  0.0 278.9 jit_solution(689007341567604600)
XLA Ops:
  6.5 0.7 all-gather.2.cloned.1.call-update
  7.3 4.6 %multiply_bitcast_fusion = f32[8,8,128,128]{3,1,2,0:T(8,128)} fusion(bf16[3,64,16384]{2,1,0:T(8,128)(2,1)} %param.14), kind=kLoop, calls=%fused_computation.5 | loop fusion | flops 3145728 | bytes 8388608
  11.9 4.9 %copy.29 = f32[8,8,128,128]{3,2,1,0:T(8,128)} copy(f32[8,8,128,128]{3,1,2,0:T(8,128)} %multiply_bitcast_fusion) | data formatting | bytes 8388608
  16.8 0.8 dynamic-slice_convert_fusion
  17.5 4.3 %fusion.1 = bf16[4,8,2,128,128]{4,3,2,0,1:T(8,128)(2,1)} fusion(f32[4,8,2,128,128]{4,3,2,1,0:T(8,128)} %bitcast.29, f32[128]{0:T(128)S(1)} %dynamic-slice_convert_fusion), kind=kLoop, calls=%fused_computation.3 | loop fusion | flops 2097152 | bytes 6291968 | tf_op jit(solution)/shard_map/convert_element_type | solution.py:257
  21.8 7.4 %all-to-all-start.1 = ((bf16[32,2,128,128]{3,2,1,0:T(8,128)(2,1)}), bf16[32,2,128,128]{3,2,1,0:T(8,128)(2,1)S(1)}, u32[]{:S(2)}, u32[]{:S(2)}) async-start(bf16[32,2,128,128]{3,2,1,0:T(8,128)(2,1)} %bitcast.3), calls=%async_computation.1 | async-start | bytes 4194304 | tf_op jit(solution)/shard_map/all_to_all | solution.py:261
  29.1 3.1 %slice.9 = bf16[1,64,16384]{2,1,0:T(8,128)(2,1)} slice(bf16[3,64,16384]{2,1,0:T(8,128)(2,1)} %param.14), slice={[0:1], [0:64], [0:16384]} | slice | bytes 4194304 | tf_op jit(solution)/shard_map/slice | solution.py:263
  32.2 0.1 dynamic_slice.7
  32.3 0.1 broadcast_in_dim.2
  32.4 0.1 broadcast_in_dim_reshape.4.gain_ref
  32.5 54.6 %all-gather.2.cloned.1.call-done = f32[1,524288]{1,0:T(1,128)} async-done(((f32[1,65536]{1,0:T(1,128)}), f32[1,524288]{1,0:T(1,128)}) %all-gather.2.cloned.1.call-update) | async-done | bytes 2097168 | tf_op jit(solution)/shard_map/all_gather | solution.py:262
  87.1 0.6 broadcast.11
  87.7 0.0 copy-start.7
  87.8 18.4 %reduce.3 = f32[524288]{0:T(1024)} reduce(f32[1,524288]{1,0:T(1,128)} %all-gather.2.cloned.1.call-done, f32[]{:T(128)} %broadcast.11), dimensions={0}, to_apply=%all_gather.3.reduce_sub_computation.3 | reduce | bytes 4194308 | tf_op jit(solution)/shard_map/all_gather | solution.py:262
  106.1 2.8 reshape.37.taps_ref
  108.9 30.5 %shard_map.136.spectrum_ref = f32[2,8192,128]{2,1,0:T(8,128)} custom-call(f32[64,8192]{1,0:T(8,128)} %reshape.37.taps_ref, bf16[256,192]{1,0:T(8,128)(2,1)S(1)} %copy-done.6, f32[2,128,128]{2,1,0:T(8,128)S(1)} %copy-done.3, f32[2,128,128]{2,1,0:T(8,128)S(1)} %copy-done.4, bf16[128,192]{1,0:T(8,128)(2,1)S(1)} %copy-done.7, bf16[768,256]{1,0:T(8,128)(2,1)S(1)} %copy-done, ...), custom_call_target="tpu_custom_call" | custom-call | flops 10000000000 | bytes 16777216 | tf_op jit(solution)/shard_map/pallas_call | solution.py:199
  139.4 4.5 %all-to-all-start = ((bf16[4,16,16384]{2,1,0:T(8,128)(2,1)}), bf16[4,16,16384]{2,1,0:T(8,128)(2,1)}, u32[]{:S(2)}, u32[]{:S(2)}) async-start(bf16[4,16,16384]{2,1,0:T(8,128)(2,1)} %bitcast), calls=%async_computation | async-start | bytes 4194304 | tf_op jit(solution)/shard_map/all_to_all | solution.py:263
  144.0 0.0 copy-start.1
  144.0 0.0 copy-start.2
  144.0 0.0 copy-start.5
  144.0 3.3 %copy.25 = bf16[2,32,128,128]{3,2,1,0:T(8,128)(2,1)} copy(bf16[2,32,128,128]{3,2,0,1:T(8,128)(2,1)} %bitcast.31) | data formatting | bytes 4194304 | tf_op jit(solution)/shard_map/transpose | solution.py:265
  147.3 4.2 %reshape.36.signal_ref = bf16[128,8192]{1,0:T(8,128)(2,1)} reshape(bf16[2,32,128,128]{3,2,1,0:T(8,128)(2,1)} %copy.25) | data formatting | bytes 4194304 | tf_op jit(solution)/shard_map/reshape | solution.py:265
  151.5 57.7 %shard_map.137 = bf16[128,8192]{1,0:T(8,128)(2,1)} custom-call(bf16[128,8192]{1,0:T(8,128)(2,1)} %reshape.36.signal_ref, f32[2,8192,128]{2,1,0:T(8,128)} %shard_map.136.spectrum_ref, f32[128,1]{1,0:T(8,128)S(1)} %broadcast_in_dim_reshape.4.gain_ref, bf16[256,256]{1,0:T(8,128)(2,1)S(1)} %copy-done.5, bf16[128,768]{1,0:T(8,128)(2,1)S(1)} %copy-done.2, ...), custom_call_target="tpu_custom_call" | custom-call | flops 20000000000 | bytes 16777216 | tf_op jit(solution)/shard_map/pallas_call | solution.py:199
  209.2 2.9 %reshape.38 = bf16[2,8,512,128]{3,2,1,0:T(8,128)(2,1)S(1)} reshape(bf16[128,8192]{1,0:T(8,128)(2,1)} %shard_map.137) | data formatting | bytes 4194304 | tf_op jit(solution)/shard_map/reshape | solution.py:271
  212.1 1.5 copy.36
  213.6 3.8 %all-to-all-start.2 = ((bf16[8,2,512,128]{3,2,1,0:T(8,128)(2,1)}), bf16[8,2,512,128]{3,2,1,0:T(8,128)(2,1)S(1)}, u32[]{:S(2)}, u32[]{:S(2)}) async-start(bf16[8,2,512,128]{3,2,1,0:T(8,128)(2,1)} %bitcast.32), calls=%async_computation.2 | async-start | bytes 4194304 | tf_op jit(solution)/shard_map/all_to_all | solution.py:272
  217.3 1.9 convert_bitcast_fusion
  219.2 2.2 copy.28
  221.5 44.7 %all-to-all-done.2 = bf16[8,2,512,128]{3,2,1,0:T(8,128)(2,1)S(1)} async-done(((bf16[8,2,512,128]{3,2,1,0:T(8,128)(2,1)}), bf16[8,2,512,128]{3,2,1,0:T(8,128)(2,1)S(1)}, u32[]{:S(2)}, u32[]{:S(2)}) %all-to-all-start.2) | async-done | bytes 2097184 | tf_op jit(solution)/shard_map/all_to_all | solution.py:272
  266.2 0.4 bitcast_convert_fusion
  266.6 1.8 copy-done.10
  268.4 3.7 %fusion = bf16[16,65536]{1,0:T(8,128)(2,1)} fusion(f32[16,65536]{1,0:T(8,128)S(1)} %bitcast.28, f32[2,8,512,128]{3,2,1,0:T(8,128)S(1)} %bitcast_convert_fusion), kind=kLoop, calls=%fused_computation.1 | loop fusion | flops 2097152 | bytes 10485760 | tf_op jit(solution)/shard_map/convert_element_type | solution.py:274
  (24 shorter events, 0.1 us)
Async XLA Ops:
  6.5 80.6 %all-gather.2.cloned.1.call-start = ((), (), s32[]{:S(2)}) async-start(), calls=%async_computation.3 | async-start | bytes 2359296 | tf_op jit(solution)/shard_map/all_gather | solution.py:262
  21.8 10.4 %copy-start.12 = (f32[16]{0:T(128)S(1)}, f32[16]{0:T(128)}, u32[]{:S(2)}) copy-start(f32[16]{0:T(128)} %param.17) | copy-start | bytes 196
  21.8 117.7 %all-to-all-start.1 = ((bf16[32,2,128,128]{3,2,1,0:T(8,128)(2,1)}), bf16[32,2,128,128]{3,2,1,0:T(8,128)(2,1)S(1)}, u32[]{:S(2)}, u32[]{:S(2)}) async-start(bf16[32,2,128,128]{3,2,1,0:T(8,128)(2,1)} %bitcast.3), calls=%async_computation.1 | async-start | bytes 4194304 | tf_op jit(solution)/shard_map/all_to_all | solution.py:261
  87.7 21.2 %copy-start = (bf16[768,256]{1,0:T(8,128)(2,1)S(1)}, bf16[768,256]{1,0:T(8,128)(2,1)}, u32[]{:S(2)}) copy-start(bf16[768,256]{1,0:T(8,128)(2,1)} %constant.55.clone.third_ref) | copy-start | bytes 1179652
  87.7 21.2 %copy-start.3 = (f32[2,128,128]{2,1,0:T(8,128)S(1)}, f32[2,128,128]{2,1,0:T(8,128)}, u32[]{:S(2)}) copy-start(f32[2,128,128]{2,1,0:T(8,128)} %constant.57.clone.start_ref) | copy-start | bytes 393220
  87.7 21.2 %copy-start.4 = (f32[2,128,128]{2,1,0:T(8,128)S(1)}, f32[2,128,128]{2,1,0:T(8,128)}, u32[]{:S(2)}) copy-start(f32[2,128,128]{2,1,0:T(8,128)} %constant.58.clone.step_ref) | copy-start | bytes 393220
  87.7 21.2 %copy-start.6 = (bf16[256,192]{1,0:T(8,128)(2,1)S(1)}, bf16[256,192]{1,0:T(8,128)(2,1)}, u32[]{:S(2)}) copy-start(bf16[256,192]{1,0:T(8,128)(2,1)} %constant.51.clone.mat_ref) | copy-start | bytes 294916
  87.7 21.2 %copy-start.7 = (bf16[128,192]{1,0:T(8,128)(2,1)S(1)}, bf16[128,192]{1,0:T(8,128)(2,1)}, u32[]{:S(2)}) copy-start(bf16[128,192]{1,0:T(8,128)(2,1)} %constant.53.clone.second_ref) | copy-start | bytes 147460
  87.7 21.2 %copy-start.8 = (f32[2,64,128]{2,1,0:T(8,128)S(1)}, f32[2,64,128]{2,1,0:T(8,128)}, u32[]{:S(2)}) copy-start(f32[2,64,128]{2,1,0:T(8,128)} %constant.59.clone.outer_ref) | copy-start | bytes 196612
  139.4 4.5 %copy-start.11 = (bf16[32,2,128,128]{3,2,1,0:T(8,128)(2,1)}, bf16[32,2,128,128]{3,2,1,0:T(8,128)(2,1)S(1)}, u32[]{:S(2)}) copy-start(bf16[32,2,128,128]{3,2,1,0:T(8,128)(2,1)S(1)} %all-to-all-done.1) | copy-start | bytes 6291460
  139.4 74.1 %all-to-all-start = ((bf16[4,16,16384]{2,1,0:T(8,128)(2,1)}), bf16[4,16,16384]{2,1,0:T(8,128)(2,1)}, u32[]{:S(2)}, u32[]{:S(2)}) async-start(bf16[4,16,16384]{2,1,0:T(8,128)(2,1)} %bitcast), calls=%async_computation | async-start | bytes 4194304 | tf_op jit(solution)/shard_map/all_to_all | solution.py:263
  144.0 7.5 %copy-start.1 = (bf16[768,256]{1,0:T(8,128)(2,1)S(1)}, bf16[768,256]{1,0:T(8,128)(2,1)}, u32[]{:S(2)}) copy-start(bf16[768,256]{1,0:T(8,128)(2,1)} %constant.56.clone.third_back_ref) | copy-start | bytes 1179652
  144.0 7.5 %copy-start.2 = (bf16[128,768]{1,0:T(8,128)(2,1)S(1)}, bf16[128,768]{1,0:T(8,128)(2,1)}, u32[]{:S(2)}) copy-start(bf16[128,768]{1,0:T(8,128)(2,1)} %constant.52.clone.last_ref) | copy-start | bytes 589828
  144.0 7.5 %copy-start.5 = (bf16[256,256]{1,0:T(8,128)(2,1)S(1)}, bf16[256,256]{1,0:T(8,128)(2,1)}, u32[]{:S(2)}) copy-start(bf16[256,256]{1,0:T(8,128)(2,1)} %constant.50.clone.mat_ref) | copy-start | bytes 393220
  144.0 7.4 %copy-start.9 = (bf16[128,192]{1,0:T(8,128)(2,1)S(1)}, bf16[128,192]{1,0:T(8,128)(2,1)}, u32[]{:S(2)}) copy-start(bf16[128,192]{1,0:T(8,128)(2,1)} %constant.54.clone.back_ref) | copy-start | bytes 147460
  213.6 52.6 %all-to-all-start.2 = ((bf16[8,2,512,128]{3,2,1,0:T(8,128)(2,1)}), bf16[8,2,512,128]{3,2,1,0:T(8,128)(2,1)S(1)}, u32[]{:S(2)}, u32[]{:S(2)}) async-start(bf16[8,2,512,128]{3,2,1,0:T(8,128)(2,1)} %bitcast.32), calls=%async_computation.2 | async-start | bytes 4194304 | tf_op jit(solution)/shard_map/all_to_all | solution.py:272
  266.2 2.2 copy-start.10
Sparse Core Ops, SparseCore 0:
  9.5 77.6 all-gather.1

commit v3 on v2

--- a/solution.py
+++ b/solution.py
@@ -42,12 +42,13 @@
     br, bi = roots(np.outer(k2, n3), Q * R)
     return {
         "first": np.concatenate(halves(np.block([[fr, -fi], [fi, fr]])), 1),
-        "taps": thrice(np.concatenate([fr, fi], 0), 1),
+        "taps": np.concatenate(halves(np.concatenate([fr, fi], 0)), 1),
         "last": thrice(np.block([[fr.T, fi.T], [-fi.T, fr.T]]) / N, 1),
         "second": thrice(np.concatenate([sr, si], 0), 1),
         "second_back": thrice(np.concatenate([sr, -si], 0), 1),
         "third": thrice(np.block([[cr, ci], [-ci, cr]]), 0),
-        "third_back": thrice(np.block([[cr, -ci], [ci, cr]]), 0),
+        "third_short": np.concatenate(halves(np.block([[cr, ci], [-ci, cr]])), 0),
+        "third_back": np.concatenate(halves(np.block([[cr, -ci], [ci, cr]])), 0),
         "start": np.stack([ar, ai]).astype(np.float32),
         "step": np.stack([gr, gi]).astype(np.float32),
         "outer": np.stack([br, bi]).astype(np.float32),
@@ -62,6 +63,11 @@
     high = x.astype(jnp.bfloat16)
     low = (x - high.astype(jnp.float32)).astype(jnp.bfloat16)
     return jnp.concatenate([high, low, high], axis)
+
+
+def twice(x, axis):
+    high = x.astype(jnp.bfloat16)
+    return jnp.concatenate([high, high], axis)
 
 
 def dot(a, b):
@@ -107,14 +113,14 @@
     return jnp.concatenate([jnp.concatenate(piece, 1) for piece in pieces], 0)
 
 
-def later_sections(src_ref, step, second_ref, third_ref, outer_ref):
+def later_sections(cut, src_ref, step, second_ref, third_ref, outer_ref):
     pieces = []
     for part in range(ROWS):
         where = pl.ds(pl.multiple_of((step * ROWS + part) * Q, Q), Q)
         pieces.append((src_ref[0, where, :], src_ref[1, where, :]))
     pieces = middle(second_ref, pieces)
     pieces = [turn(re, im, outer_ref[0], outer_ref[1]) for re, im in pieces]
-    return dot(split(lanes(pieces), 1), third_ref[...])
+    return dot(cut(lanes(pieces), 1), third_ref[...])
 
 
 def block(step):
@@ -122,15 +128,23 @@
 
 
 def taps_kernel(
-    taps_ref, mat_ref, start_ref, step_ref, second_ref, third_ref, outer_ref, out_ref, held
+    taps_ref, mat_ref, start_ref, step_ref, second_ref, third_ref, outer_ref, out_ref, held, wide
 ):
+    def widen(step, carry):
+        where = pl.ds(pl.multiple_of(step * 512, 512), 512)
+        wide[where, :] = taps_ref[where, :].astype(jnp.float32)
+        return carry
+
+    lax.fori_loop(0, HALF * Q // 512, widen, 0)
+
     def load(step):
-        return split(taps_ref[:, columns(step)], 0)
+        found = [wide[pl.ds(step * WIDE + part, HALF, stride=Q), :] for part in range(WIDE)]
+        return twice(jnp.concatenate(found, 1), 0)
 
     first_section(load, mat_ref, start_ref, step_ref, held)
 
     def one(step, carry):
-        flat = later_sections(held, step, second_ref, third_ref, outer_ref)
+        flat = later_sections(split, held, step, second_ref, third_ref, outer_ref)
         out_ref[0, block(step), :] = flat[:, :R]
         out_ref[1, block(step), :] = flat[:, R:]
         return carry
@@ -153,19 +167,37 @@
     outer_ref,
     out_ref,
     held,
+    wide,
 ):
+    sources, _, rows, _ = signal_ref.shape
+    targets, _, span, _ = out_ref.shape
+
+    def widen(step, carry):
+        where = pl.ds(pl.multiple_of(step * rows, rows), rows)
+        for part in range(2):
+            wide[part, where, :] = signal_ref[step, part].astype(jnp.float32)
+        return carry
+
+    lax.fori_loop(0, sources, widen, 0)
+
+    def digits(number):
+        return pl.ds(number, HALF, stride=Q)
+
     def load(step):
-        part = signal_ref[:, columns(step)]
-        return jnp.concatenate([part, part], 0)
+        found = []
+        for part in range(WIDE):
+            where = digits(step * WIDE + part)
+            found.append(jnp.concatenate([wide[0, where, :], wide[1, where, :]], 0))
+        return twice(jnp.concatenate(found, 1), 0)
 
     first_section(load, mat_ref, start_ref, step_ref, held)
 
     def one(step, carry):
-        flat = later_sections(held, step, second_ref, third_ref, outer_ref)
+        flat = later_sections(twice, held, step, second_ref, third_ref, outer_ref)
         re, im = turn(
             flat[:, :R], flat[:, R:], spectrum_ref[0, block(step), :], spectrum_ref[1, block(step), :]
         )
-        flat = dot(split(jnp.concatenate([re, im], 1), 1), third_back_ref[...])
+        flat = dot(twice(jnp.concatenate([re, im], 1), 1), third_back_ref[...])
         pieces = []
         for part in range(ROWS):
             piece = flat[part * Q : (part + 1) * Q]
@@ -188,20 +220,74 @@
             found.append(jnp.concatenate([re, im], 0))
             wr, wi = turn(wr, wi, step_ref[0], step_ref[1])
         flat = dot(last_ref[...], split(jnp.concatenate(found, 1), 0))
-        direct = gain_ref[...] * signal_ref[:, columns(step)].astype(jnp.float32)
-        out_ref[:, columns(step)] = (flat + direct).astype(jnp.bfloat16)
+        for part in range(WIDE):
+            where = digits(step * WIDE + part)
+            for half in range(2):
+                piece = flat[half * HALF : (half + 1) * HALF, part * R : (part + 1) * R]
+                wide[half, where, :] = piece + gain_ref[half] * wide[half, where, :]
         return wr, wi
 
     lax.fori_loop(0, Q // WIDE, finish, (start_ref[0], start_ref[1]))
 
-
-def run(kernel, out_shape, out_dtype, flops, *operands):
+    def narrow(step, carry):
+        where = pl.ds(pl.multiple_of(step * span, span), span)
+        for part in range(2):
+            out_ref[step, part] = wide[part, where, :].astype(jnp.bfloat16)
+        return carry
+
+    lax.fori_loop(0, targets, narrow, 0)
+
+
+def product_kernel(keep_ref, key_ref, value_ref, out_ref, wide):
+    pairs, _, _, sub, _ = out_ref.shape
+    rows = 2 * pairs
+
+    def one(step, carry):
+        for part in range(8):
+            at = step * 8 + part
+            where = pl.ds(pl.multiple_of(at * R, R), R)
+            keep = keep_ref[at].astype(jnp.float32)
+            found = key_ref[:, where].astype(jnp.float32) * value_ref[:, where].astype(jnp.float32)
+            wide[pl.ds(at, rows, stride=sub), :] = found * keep
+        return carry
+
+    lax.fori_loop(0, sub // 8, one, 0)
+    for row in range(rows):
+        out_ref[row // 2, 0, row % 2] = wide[row * sub : (row + 1) * sub, :].astype(jnp.bfloat16)
+
+
+def multiply(keep, projected, chan, pairs):
+    sub = keep.shape[0]
+    here = sub * R
+
+    def rows_of(which):
+        return pl.BlockSpec((None, 2 * pairs, here), lambda at: (which, at, 0))
+
+    return pl.pallas_call(
+        product_kernel,
+        grid=(chan,),
+        out_shape=jax.ShapeDtypeStruct((pairs, chan, 2, sub, R), jnp.bfloat16),
+        in_specs=[pl.BlockSpec(memory_space=pltpu.SMEM), rows_of(1), rows_of(2)],
+        out_specs=pl.BlockSpec((pairs, 1, 2, sub, R), lambda at: (0, at, 0, 0, 0)),
+        scratch_shapes=[pltpu.VMEM((2 * pairs * sub, R), jnp.float32)],
+        compiler_params=pltpu.CompilerParams(vmem_limit_bytes=24 * 1024 * 1024),
+        cost_estimate=pl.CostEstimate(
+            flops=4 * chan * pairs * here, bytes_accessed=12 * chan * pairs * here, transcendentals=0
+        ),
+    )(keep, projected, projected)
+
+
+def run(kernel, out_shape, out_dtype, flops, wide_shape, scalars, *operands):
+    spaces = [pltpu.SMEM if at in scalars else pltpu.VMEM for at in range(len(operands))]
     return pl.pallas_call(
         kernel,
         out_shape=jax.ShapeDtypeStruct(out_shape, out_dtype),
-        in_specs=[pl.BlockSpec(memory_space=pltpu.VMEM)] * len(operands),
+        in_specs=[pl.BlockSpec(memory_space=space) for space in spaces],
         out_specs=pl.BlockSpec(memory_space=pltpu.VMEM),
-        scratch_shapes=[pltpu.VMEM((2, P1 * Q, R), jnp.float32)],
+        scratch_shapes=[
+            pltpu.VMEM((2, P1 * Q, R), jnp.float32),
+            pltpu.VMEM(wide_shape, jnp.float32),
+        ],
         compiler_params=pltpu.CompilerParams(vmem_limit_bytes=52 * 1024 * 1024),
         cost_estimate=pl.CostEstimate(
             flops=flops, bytes_accessed=16 * 1024 * 1024, transcendentals=0
@@ -212,11 +298,18 @@
 def transform_taps(taps, tabs):
     names = ("taps", "start", "step", "second", "third", "outer")
     return run(
-        taps_kernel, (2, P1 * Q, R), jnp.float32, 10**10, taps, *[tabs[name] for name in names]
+        taps_kernel,
+        (2, P1 * Q, R),
+        jnp.float32,
+        10**10,
+        (HALF * Q, R),
+        (),
+        taps,
+        *[tabs[name] for name in names],
     )
 
 
-def convolve(signal, spectrum, gain, tabs):
+def convolve(signal, spectrum, gain, targets, tabs):
     names = (
         "first",
         "last",
@@ -224,16 +317,18 @@
         "step",
         "second",
         "second_back",
-        "third",
+        "third_short",
         "third_back",
         "outer",
     )
     operands = [tabs[name] for name in names]
     return run(
         signal_kernel,
-        (2 * HALF, Q * R),
+        (targets, 2, HALF * Q // targets, R),
         jnp.bfloat16,
         2 * 10**10,
+        (2, HALF * Q, R),
+        (2,),
         signal,
         spectrum,
         gain,
@@ -250,25 +345,18 @@
     copies = seq // pairs
     sub = live_blocks.shape[0] // chan
     span = here * chan
-    keep = lax.dynamic_slice_in_dim(live_blocks, at_chan * sub, sub).astype(jnp.float32)
-    keep = jnp.broadcast_to(keep[:, None], (sub, R)).reshape(1, here)
-    product = (
-        projected[1].astype(jnp.float32) * projected[2].astype(jnp.float32) * keep
-    ).astype(jnp.bfloat16)
-    rows = product.reshape(chan, pairs, 2, here // R, R)
-    rows = jnp.repeat(rows, copies, axis=1) if copies > 1 else rows
-    rows = rows.transpose(1, 0, 2, 3, 4).reshape(seq * chan, 2, here // R, R)
+    keep = lax.dynamic_slice_in_dim(live_blocks, at_chan * sub, sub)
+    rows = multiply(keep, projected, chan, pairs)
+    rows = jnp.repeat(rows, copies, axis=0) if copies > 1 else rows
+    rows = rows.reshape(seq * chan, 2, here // R, R)
     rows = lax.all_to_all(rows, ("seq", "chan"), split_axis=0, concat_axis=0, tiled=True)
-    taps = lax.all_gather(filters, "seq", axis=1, tiled=True)
+    taps = filters.astype(jnp.bfloat16).reshape(span // R, R)
+    taps = lax.all_gather(taps, "seq", axis=0, tiled=True)
     gate = lax.all_to_all(projected[0], "chan", split_axis=0, concat_axis=1, tiled=True)
     tabs = {name: jnp.asarray(table) for name, table in tables().items()}
-    signal = rows.transpose(1, 0, 2, 3).reshape(2 * HALF, Q * R)
-    spectrum = transform_taps(taps.reshape(HALF, Q * R), tabs)
-    pair = at_seq // copies
-    gain = lax.dynamic_slice_in_dim(skip_gain, 2 * pair, 2)
-    gain = jnp.repeat(gain, HALF)[:, None]
-    summed = convolve(signal, spectrum, gain, tabs)
-    summed = summed.reshape(2, seq, span // R, R).transpose(1, 0, 2, 3)
+    spectrum = transform_taps(taps, tabs)
+    gain = lax.dynamic_slice_in_dim(skip_gain, 2 * (at_seq // copies), 2)
+    summed = convolve(rows, spectrum, gain, seq, tabs)
     summed = lax.all_to_all(summed, "seq", split_axis=0, concat_axis=0, tiled=True)
     summed = summed[::copies].reshape(own, span)
     return (gate.astype(jnp.float32) * summed.astype(jnp.float32)).astype(jnp.bfloat16)

time: 280 us -> 242 us (0.86)
  other arithmetic: 34 us -> 7.48 us
  local copies, waits for them, and re-layouts: 27.4 us -> 12.1 us
  Pallas kernels: 88.2 us -> 95 us
    all_gather x1 -> x0, other arithmetic: 18.4 us -> none  [body(): taps = lax.all_gather(filters, 'seq', axis=1, tiled=True)]
    reshape x4 -> x0, local copies, waits for them, and re-layouts: 11.3 us -> none  [the longest x2 4.38 us: body(): summed = summed.reshape(2, seq, span // R, R).transpose(1, 0, 2, 3)]
    pallas_call x0 -> x1, Pallas kernels: none -> 5.65 us  [multiply(): pl.pallas_call(product_kernel, grid=(chan,), out_shape=jax.ShapeDtypeStru...]
    unnamed x3 -> x2, other arithmetic: 6.9 us -> 2.43 us
    convert_element_type x2 -> x1, other arithmetic: 5.01 us -> 1.34 us  [body(): taps = filters.astype(jnp.bfloat16).reshape(span // R, R)]
    all_gather x1, waiting for transfers between devices: 54.6 us -> 51.2 us  [body(): taps = lax.all_gather(taps, 'seq', axis=0, tiled=True)]
    transpose x1 -> x0, local copies, waits for them, and re-layouts: 3.26 us -> none  [body(): signal = rows.transpose(1, 0, 2, 3).reshape(2 * HALF, Q * R)]
    unnamed x27 -> x34, local copies, waits for them, and re-layouts: 6.72 us -> 6.05 us
  transfers between devices with their start and end apart: 4 -> 4, of which waited for: 2 -> 2; matrix products, arithmetic and copies ran while one was open for 20% -> 3% of each run, Pallas kernels for 32% -> 37%
where the time goes in v3:
time: 242 us; the launch traced here: 241 us
  waiting for transfers between devices  97.9 us (40%)
  Pallas kernels  95 us (39%)
  starting transfers between devices  15.3 us (6%)
  between operations  13.6 us (6%)
  local copies, waits for them, and re-layouts  12.1 us (5%)
  other arithmetic  7.48 us (3%)
    pallas_call x2, Pallas kernels, run(): pl.pallas_call(kernel, out_shape=jax.ShapeDtypeStruct(out_shape, out_dtyp...  89.3 us
    all_gather x1, waiting for transfers between devices, body(): taps = lax.all_gather(taps, 'seq', axis=0, tiled=True)  51.2 us
    all_to_all x1, waiting for transfers between devices, body(): lax.all_to_all(summed, 'seq', split_axis=0, concat_axis=0, tiled=True)  46.6 us
    all_to_all x1, starting transfers between devices, body(): lax.all_to_all(rows, ('seq', 'chan'), split_axis=0, concat_axis=0, tiled=...  7.3 us
    unnamed x34, local copies, waits for them, and re-layouts  6.05 us
    pallas_call x1, Pallas kernels, multiply(): pl.pallas_call(product_kernel, grid=(chan,), out_shape=jax.ShapeDtypeStru...  5.65 us
  transfers between devices with their start and end apart: 4, of which 2 were waited for; matrix products, arithmetic and copies ran while one was open for 3% of the time, Pallas kernels for 37%

profile of v3, /device:TPU:0, one launch (start us, length us, event | category | flops | bytes accessed | tf_op | source)
XLA Modules:
  0.0 241.4 jit_solution(1802959760204023827)
XLA Ops:
  6.5 0.8 dynamic_slice.6.keep_ref
  7.3 2.8 %copy-done = bf16[3,64,16384]{2,1,0:T(8,128)(2,1)S(1)} copy-done((bf16[3,64,16384]{2,1,0:T(8,128)(2,1)S(1)}, bf16[3,64,16384]{2,1,0:T(8,128)(2,1)}, u32[]{:S(2)}) %copy-start) | copy-done | bytes 6291480
  10.1 5.7 %shard_map.145 = bf16[8,4,2,128,128]{4,3,2,1,0:T(8,128)(2,1)} custom-call(s32[128]{0:T(128)S(1)} %dynamic_slice.6.keep_ref, bf16[3,64,16384]{2,1,0:T(8,128)(2,1)S(1)} %copy-done, bf16[3,64,16384]{2,1,0:T(8,128)(2,1)S(1)} %copy-done), custom_call_target="tpu_custom_call" | custom-call | flops 2097152 | bytes 6291456 | tf_op jit(solution)/shard_map/pallas_call | solution.py:266
  15.7 0.0 copy-start.7
  15.8 0.0 copy-start.9
  15.8 0.0 copy-start.10
  15.8 0.0 copy-start.12
  15.8 7.3 %all-to-all-start.1 = ((bf16[32,2,128,128]{3,2,1,0:T(8,128)(2,1)}), bf16[32,2,128,128]{3,2,1,0:T(8,128)(2,1)S(1)}, u32[]{:S(2)}, u32[]{:S(2)}) async-start(bf16[32,2,128,128]{3,2,1,0:T(8,128)(2,1)} %bitcast.2), calls=%async_computation.1 | async-start | bytes 4194304 | tf_op jit(solution)/shard_map/all_to_all | solution.py:352
  23.1 0.0 all-gather.2.cloned.1.call-start
  23.2 1.3 convert_reduce_fusion
  24.5 0.0 all-gather.2.cloned.1.call-update
  24.5 3.0 %slice.3 = bf16[1,64,16384]{2,1,0:T(8,128)(2,1)} slice(bf16[3,64,16384]{2,1,0:T(8,128)(2,1)} %value_ref.1), slice={[0:1], [0:64], [0:16384]} | slice | bytes 4194304 | tf_op jit(solution)/shard_map/slice | solution.py:355
  27.6 0.1 dynamic_slice.7.gain_ref
  27.7 51.2 %all-gather.2.cloned.1.call-done.taps_ref = bf16[4096,128]{1,0:T(8,128)(2,1)} async-done(((bf16[512,128]{1,0:T(8,128)(2,1)}), bf16[4096,128]{1,0:T(8,128)(2,1)}) %all-gather.2.cloned.1.call-update) | async-done | bytes 1048592 | tf_op jit(solution)/shard_map/all_gather | solution.py:354
  78.9 0.0 copy-done.2
  78.9 0.0 copy-done.10
  78.9 0.0 copy-done.12
  78.9 1.2 copy-done.1
  80.1 30.0 %shard_map.146.spectrum_ref = f32[2,8192,128]{2,1,0:T(8,128)} custom-call(bf16[4096,128]{1,0:T(8,128)(2,1)S(1)} %copy-done.1, bf16[256,128]{1,0:T(8,128)(2,1)S(1)} %copy-done.12, f32[2,128,128]{2,1,0:T(8,128)S(1)} %copy-done.6, f32[2,128,128]{2,1,0:T(8,128)S(1)} %copy-done.7, bf16[128,192]{1,0:T(8,128)(2,1)S(1)} %copy-done.9, ...), custom_call_target="tpu_custom_call" | custom-call | flops 10000000000 | bytes 16777216 | tf_op jit(solution)/shard_map/pallas_call | solution.py:282
  110.1 0.0 copy-start.11
  110.1 0.0 all-to-all-done.1.signal_ref
  110.1 1.3 copy-done.14
  111.5 3.6 %all-to-all-start = ((bf16[4,16,16384]{2,1,0:T(8,128)(2,1)}), bf16[4,16,16384]{2,1,0:T(8,128)(2,1)S(1)}, u32[]{:S(2)}, u32[]{:S(2)}) async-start(bf16[4,16,16384]{2,1,0:T(8,128)(2,1)} %bitcast.17), calls=%async_computation | async-start | bytes 4194304 | tf_op jit(solution)/shard_map/all_to_all | solution.py:355
  115.1 59.4 %shard_map.147 = bf16[8,2,512,128]{3,2,1,0:T(8,128)(2,1)} custom-call(bf16[32,2,128,128]{3,2,1,0:T(8,128)(2,1)} %copy-done.14, f32[2,8192,128]{2,1,0:T(8,128)} %shard_map.146.spectrum_ref, f32[2]{0:T(128)S(1)} %dynamic_slice.7.gain_ref, bf16[256,256]{1,0:T(8,128)(2,1)S(1)} %copy-done.8, bf16[128,768]{1,0:T(8,128)(2,1)S(1)} %copy-done.5, ...), custom_call_target="tpu_custom_call" | custom-call | flops 20000000000 | bytes 16777216 | tf_op jit(solution)/shard_map/pallas_call | solution.py:282
  174.5 0.0 all-to-all-done
  174.5 4.4 %all-to-all-start.2 = ((bf16[8,2,512,128]{3,2,1,0:T(8,128)(2,1)}), bf16[8,2,512,128]{3,2,1,0:T(8,128)(2,1)}, u32[]{:S(2)}, u32[]{:S(2)}) async-start(bf16[8,2,512,128]{3,2,1,0:T(8,128)(2,1)} %shard_map.147), calls=%async_computation.2 | async-start | bytes 4194304 | tf_op jit(solution)/shard_map/all_to_all | solution.py:360
  178.9 0.3 convert_bitcast_fusion
  179.1 2.2 copy.18
  181.4 46.6 %all-to-all-done.2 = bf16[8,2,512,128]{3,2,1,0:T(8,128)(2,1)} async-done(((bf16[8,2,512,128]{3,2,1,0:T(8,128)(2,1)}), bf16[8,2,512,128]{3,2,1,0:T(8,128)(2,1)}, u32[]{:S(2)}, u32[]{:S(2)}) %all-to-all-start.2) | async-done | bytes 2097184 | tf_op jit(solution)/shard_map/all_to_all | solution.py:360
  228.0 2.2 bitcast_convert_fusion
  230.2 0.7 copy-done.13
  230.8 3.7 %fusion = bf16[16,65536]{1,0:T(8,128)(2,1)} fusion(f32[16,65536]{1,0:T(8,128)S(1)} %bitcast.16, f32[2,8,512,128]{3,2,1,0:T(8,128)S(1)} %bitcast_convert_fusion), kind=kLoop, calls=%fused_computation.1 | loop fusion | flops 2097152 | bytes 10485760 | tf_op jit(solution)/shard_map/convert_element_type | solution.py:362
  (22 shorter events, 0.0 us)
Async XLA Ops:
  7.3 2.8 %copy-start = (bf16[3,64,16384]{2,1,0:T(8,128)(2,1)S(1)}, bf16[3,64,16384]{2,1,0:T(8,128)(2,1)}, u32[]{:S(2)}) copy-start(bf16[3,64,16384]{2,1,0:T(8,128)(2,1)} %value_ref.1) | copy-start | bytes 18874372
  15.7 7.4 %copy-start.15 = (f32[1,65536]{1,0:T(1,128)S(1)}, f32[1,65536]{1,0:T(1,128)}, u32[]{:S(2)}) copy-start(f32[1,65536]{1,0:T(1,128)} %param.17) | copy-start | bytes 786436
  15.7 11.8 %copy-start.16 = (f32[16]{0:T(128)S(1)}, f32[16]{0:T(128)}, u32[]{:S(2)}) copy-start(f32[16]{0:T(128)} %param.18) | copy-start | bytes 196
  15.7 63.1 %copy-start.2 = (bf16[768,256]{1,0:T(8,128)(2,1)S(1)}, bf16[768,256]{1,0:T(8,128)(2,1)}, u32[]{:S(2)}) copy-start(bf16[768,256]{1,0:T(8,128)(2,1)} %constant.57.clone.third_ref) | copy-start | bytes 1179652
  15.7 63.1 %copy-start.6 = (f32[2,128,128]{2,1,0:T(8,128)S(1)}, f32[2,128,128]{2,1,0:T(8,128)}, u32[]{:S(2)}) copy-start(f32[2,128,128]{2,1,0:T(8,128)} %constant.60.clone.start_ref) | copy-start | bytes 393220
  15.7 63.1 %copy-start.7 = (f32[2,128,128]{2,1,0:T(8,128)S(1)}, f32[2,128,128]{2,1,0:T(8,128)}, u32[]{:S(2)}) copy-start(f32[2,128,128]{2,1,0:T(8,128)} %constant.61.clone.step_ref) | copy-start | bytes 393220
  15.8 63.1 %copy-start.9 = (bf16[128,192]{1,0:T(8,128)(2,1)S(1)}, bf16[128,192]{1,0:T(8,128)(2,1)}, u32[]{:S(2)}) copy-start(bf16[128,192]{1,0:T(8,128)(2,1)} %constant.55.clone.second_ref) | copy-start | bytes 147460
  15.8 63.1 %copy-start.10 = (f32[2,64,128]{2,1,0:T(8,128)S(1)}, f32[2,64,128]{2,1,0:T(8,128)}, u32[]{:S(2)}) copy-start(f32[2,64,128]{2,1,0:T(8,128)} %constant.62.clone.outer_ref) | copy-start | bytes 196612
  15.8 63.1 %copy-start.12 = (bf16[256,128]{1,0:T(8,128)(2,1)S(1)}, bf16[256,128]{1,0:T(8,128)(2,1)}, u32[]{:S(2)}) copy-start(bf16[256,128]{1,0:T(8,128)(2,1)} %constant.53.clone.mat_ref) | copy-start | bytes 196612
  15.8 94.3 %all-to-all-start.1 = ((bf16[32,2,128,128]{3,2,1,0:T(8,128)(2,1)}), bf16[32,2,128,128]{3,2,1,0:T(8,128)(2,1)S(1)}, u32[]{:S(2)}, u32[]{:S(2)}) async-start(bf16[32,2,128,128]{3,2,1,0:T(8,128)(2,1)} %bitcast.2), calls=%async_computation.1 | async-start | bytes 4194304 | tf_op jit(solution)/shard_map/all_to_all | solution.py:352
  23.1 55.8 %all-gather.2.cloned.1.call-start = ((), (), s32[]{:S(2)}) async-start(), calls=%async_computation.3 | async-start | bytes 1179648 | tf_op jit(solution)/shard_map/all_gather | solution.py:354
  78.9 1.2 copy-start.1
  110.1 5.0 %copy-start.3 = (bf16[512,256]{1,0:T(8,128)(2,1)S(1)}, bf16[512,256]{1,0:T(8,128)(2,1)}, u32[]{:S(2)}) copy-start(bf16[512,256]{1,0:T(8,128)(2,1)} %constant.58.clone.third_ref) | copy-start | bytes 786436
  110.1 5.0 %copy-start.4 = (bf16[512,256]{1,0:T(8,128)(2,1)S(1)}, bf16[512,256]{1,0:T(8,128)(2,1)}, u32[]{:S(2)}) copy-start(bf16[512,256]{1,0:T(8,128)(2,1)} %constant.59.clone.third_back_ref) | copy-start | bytes 786436
  110.1 5.0 %copy-start.5 = (bf16[128,768]{1,0:T(8,128)(2,1)S(1)}, bf16[128,768]{1,0:T(8,128)(2,1)}, u32[]{:S(2)}) copy-start(bf16[128,768]{1,0:T(8,128)(2,1)} %constant.54.clone.last_ref) | copy-start | bytes 589828
  110.1 5.0 %copy-start.8 = (bf16[256,256]{1,0:T(8,128)(2,1)S(1)}, bf16[256,256]{1,0:T(8,128)(2,1)}, u32[]{:S(2)}) copy-start(bf16[256,256]{1,0:T(8,128)(2,1)} %constant.52.clone.mat_ref) | copy-start | bytes 393220
  110.1 5.0 %copy-start.11 = (bf16[128,192]{1,0:T(8,128)(2,1)S(1)}, bf16[128,192]{1,0:T(8,128)(2,1)}, u32[]{:S(2)}) copy-start(bf16[128,192]{1,0:T(8,128)(2,1)} %constant.56.clone.back_ref) | copy-start | bytes 147460
  110.1 1.3 copy-start.14
  111.5 63.0 %all-to-all-start = ((bf16[4,16,16384]{2,1,0:T(8,128)(2,1)}), bf16[4,16,16384]{2,1,0:T(8,128)(2,1)S(1)}, u32[]{:S(2)}, u32[]{:S(2)}) async-start(bf16[4,16,16384]{2,1,0:T(8,128)(2,1)} %bitcast.17), calls=%async_computation | async-start | bytes 4194304 | tf_op jit(solution)/shard_map/all_to_all | solution.py:355
  174.5 53.5 %all-to-all-start.2 = ((bf16[8,2,512,128]{3,2,1,0:T(8,128)(2,1)}), bf16[8,2,512,128]{3,2,1,0:T(8,128)(2,1)}, u32[]{:S(2)}, u32[]{:S(2)}) async-start(bf16[8,2,512,128]{3,2,1,0:T(8,128)(2,1)} %shard_map.147), calls=%async_computation.2 | async-start | bytes 4194304 | tf_op jit(solution)/shard_map/all_to_all | solution.py:360
  228.0 2.8 %copy-start.13 = (f32[4,2,8,16384]{3,2,0,1:T(8,128)S(1)}, f32[4,2,8,16384]{3,2,0,1:T(8,128)}, u32[]{:S(2)}) copy-start(f32[4,2,8,16384]{3,2,0,1:T(8,128)} %copy.18) | copy-start | bytes 12582916
Sparse Core Ops, SparseCore 0:
  26.1 52.7 all-gather.1

commit v4 on v3

--- a/solution.py
+++ b/solution.py
@@ -74,8 +74,8 @@
     return jnp.dot(a, b, preferred_element_type=jnp.float32)
 
 
-WIDE = 4
-ROWS = 4
+WIDE = 8
+ROWS = 8
 
 
 def columns(step):
@@ -275,6 +275,57 @@
             flops=4 * chan * pairs * here, bytes_accessed=12 * chan * pairs * here, transcendentals=0
         ),
     )(keep, projected, projected)
+
+
+def follow_kernel(value_ref, earlier_ref, out_ref):
+    del value_ref, earlier_ref, out_ref
+
+
+def follow(value, earlier):
+    return pl.pallas_call(
+        follow_kernel,
+        out_shape=jax.ShapeDtypeStruct(value.shape, value.dtype),
+        in_specs=[pl.BlockSpec(memory_space=pl.ANY)] * 2,
+        out_specs=pl.BlockSpec(memory_space=pl.ANY),
+        input_output_aliases={0: 0},
+    )(value, earlier)
+
+
+def gate_kernel(gate_ref, summed_ref, out_ref, wide):
+    pairs, _, sub, _ = summed_ref.shape
+    rows = 2 * pairs
+    for row in range(rows):
+        wide[row * sub : (row + 1) * sub, :] = summed_ref[row // 2, row % 2].astype(jnp.float32)
+
+    def one(step, carry):
+        for part in range(8):
+            at = step * 8 + part
+            where = pl.ds(pl.multiple_of(at * R, R), R)
+            found = gate_ref[:, where].astype(jnp.float32) * wide[pl.ds(at, rows, stride=sub), :]
+            out_ref[:, where] = found.astype(jnp.bfloat16)
+        return carry
+
+    lax.fori_loop(0, sub // 8, one, 0)
+
+
+def apply_gate(gate, summed):
+    chan, own, here = gate.shape
+    pairs, sub = summed.shape[0], here // R
+    return pl.pallas_call(
+        gate_kernel,
+        grid=(chan,),
+        out_shape=jax.ShapeDtypeStruct((own, chan * here), jnp.bfloat16),
+        in_specs=[
+            pl.BlockSpec((None, own, here), lambda at: (at, 0, 0)),
+            pl.BlockSpec((pairs, 2, sub, R), lambda at: (0, 0, at, 0)),
+        ],
+        out_specs=pl.BlockSpec((own, here), lambda at: (0, at)),
+        scratch_shapes=[pltpu.VMEM((own * sub, R), jnp.float32)],
+        compiler_params=pltpu.CompilerParams(vmem_limit_bytes=24 * 1024 * 1024),
+        cost_estimate=pl.CostEstimate(
+            flops=2 * chan * own * here, bytes_accessed=6 * chan * own * here, transcendentals=0
+        ),
+    )(gate, summed)
 
 
 def run(kernel, out_shape, out_dtype, flops, wide_shape, scalars, *operands):
@@ -349,17 +400,19 @@
     rows = multiply(keep, projected, chan, pairs)
     rows = jnp.repeat(rows, copies, axis=0) if copies > 1 else rows
     rows = rows.reshape(seq * chan, 2, here // R, R)
-    rows = lax.all_to_all(rows, ("seq", "chan"), split_axis=0, concat_axis=0, tiled=True)
     taps = filters.astype(jnp.bfloat16).reshape(span // R, R)
     taps = lax.all_gather(taps, "seq", axis=0, tiled=True)
-    gate = lax.all_to_all(projected[0], "chan", split_axis=0, concat_axis=1, tiled=True)
+    rows = follow(rows, taps)
+    rows = lax.all_to_all(rows, ("seq", "chan"), split_axis=0, concat_axis=0, tiled=True)
+    gate = lax.all_to_all(
+        projected[0].reshape(chan, own, here), "chan", split_axis=0, concat_axis=0, tiled=True
+    )
     tabs = {name: jnp.asarray(table) for name, table in tables().items()}
     spectrum = transform_taps(taps, tabs)
     gain = lax.dynamic_slice_in_dim(skip_gain, 2 * (at_seq // copies), 2)
     summed = convolve(rows, spectrum, gain, seq, tabs)
     summed = lax.all_to_all(summed, "seq", split_axis=0, concat_axis=0, tiled=True)
-    summed = summed[::copies].reshape(own, span)
-    return (gate.astype(jnp.float32) * summed.astype(jnp.float32)).astype(jnp.bfloat16)
+    return apply_gate(gate, summed[::copies])
 
 
 def solution(mesh):

time: 242 us -> 220 us (0.909)
  blocking collectives: 0 us -> 52.6 us
  waiting for transfers between devices: 97.9 us -> 56.9 us
  Pallas kernels: 95 us -> 78.4 us
  starting transfers between devices: 15.3 us -> 7.25 us
  other arithmetic: 7.48 us -> 2.28 us
  local copies, waits for them, and re-layouts: 12.1 us -> 8.19 us
    all_to_all x0 -> x1, blocking collectives: none -> 52.6 us  [body(): lax.all_to_all(summed, 'seq', split_axis=0, concat_axis=0, tiled=True)]
    all_to_all x2 -> x1, waiting for transfers between devices: 46.6 us -> 0.01 us  [body(): lax.all_to_all(projected[0].reshape(chan, own, here), 'chan', split_axis=...]
    all_to_all x1, waiting for transfers between devices: 0.01 us -> 23.3 us  [body(): lax.all_to_all(rows, ('seq', 'chan'), split_axis=0, concat_axis=0, tiled=...]
    pallas_call x2, Pallas kernels: 89.3 us -> 69 us  [run(): pl.pallas_call(kernel, out_shape=jax.ShapeDtypeStruct(out_shape, out_dtyp...]
    all_gather x1, waiting for transfers between devices: 51.2 us -> 33.6 us  [body(): taps = lax.all_gather(taps, 'seq', axis=0, tiled=True)]
    pallas_call x0 -> x2, Pallas kernels: none -> 4.41 us  [the longest x1 4.41 us: apply_gate(): pl.pallas_call(gate_kernel, grid=(chan,), out_shape=jax.ShapeDtypeStruct(...]
    all_to_all x2 -> x1, starting transfers between devices: 7.97 us -> 3.75 us  [body(): lax.all_to_all(projected[0].reshape(chan, own, here), 'chan', split_axis=...]
    all_to_all x1, starting transfers between devices: 7.3 us -> 3.49 us  [body(): lax.all_to_all(rows, ('seq', 'chan'), split_axis=0, concat_axis=0, tiled=...]
  transfers between devices with their start and end apart: 4 -> 3, of which waited for: 2 -> 2; matrix products, arithmetic and copies ran while one was open for 3% -> 2% of each run, Pallas kernels for 37% -> 34%
where the time goes in v4:
time: 220 us; the launch traced here: 219 us
  Pallas kernels  78.4 us (36%)
  waiting for transfers between devices  56.9 us (26%)
  blocking collectives  52.6 us (24%)
  between operations  13.6 us (6%)
  local copies, waits for them, and re-layouts  8.19 us (4%)
  starting transfers between devices  7.25 us (3%)
  other arithmetic  2.28 us (1%)
    pallas_call x2, Pallas kernels, run(): pl.pallas_call(kernel, out_shape=jax.ShapeDtypeStruct(out_shape, out_dtyp...  69 us
    all_to_all x1, blocking collectives, body(): lax.all_to_all(summed, 'seq', split_axis=0, concat_axis=0, tiled=True)  52.6 us
    all_gather x1, waiting for transfers between devices, body(): taps = lax.all_gather(taps, 'seq', axis=0, tiled=True)  33.6 us
    all_to_all x1, waiting for transfers between devices, body(): lax.all_to_all(rows, ('seq', 'chan'), split_axis=0, concat_axis=0, tiled=...  23.3 us
    pallas_call x1, Pallas kernels, multiply(): pl.pallas_call(product_kernel, grid=(chan,), out_shape=jax.ShapeDtypeStru...  4.98 us
    pallas_call x1, Pallas kernels, apply_gate(): pl.pallas_call(gate_kernel, grid=(chan,), out_shape=jax.ShapeDtypeStruct(...  4.41 us
  transfers between devices with their start and end apart: 3, of which 2 were waited for; matrix products, arithmetic and copies ran while one was open for 2% of the time, Pallas kernels for 34%

profile of v4, /device:TPU:0, one launch (start us, length us, event | category | flops | bytes accessed | tf_op | source)
XLA Modules:
  0.0 219.2 jit_solution(11510528637412600788)
XLA Ops:
  6.5 0.0 all-gather.2.cloned.1.call-start
  6.5 2.3 %convert_reduce_fusion = bf16[65536]{0:T(1024)(128)(2,1)} fusion(f32[1,65536]{1,0:T(1,128)} %param.17), kind=kLoop, calls=%fused_computation | loop fusion | flops 65536 | bytes 393216 | tf_op jit(solution)/shard_map/convert_element_type | solution.py:403
  8.8 0.0 all-gather.2.cloned.1.call-update
  8.8 0.8 dynamic_slice.6.keep_ref
  9.6 2.8 %copy-done = bf16[3,64,16384]{2,1,0:T(8,128)(2,1)S(1)} copy-done((bf16[3,64,16384]{2,1,0:T(8,128)(2,1)S(1)}, bf16[3,64,16384]{2,1,0:T(8,128)(2,1)}, u32[]{:S(2)}) %copy-start) | copy-done | bytes 6291480
  12.4 5.0 %shard_map.145 = bf16[8,4,2,128,128]{4,3,2,1,0:T(8,128)(2,1)S(1)} custom-call(s32[128]{0:T(128)S(1)} %dynamic_slice.6.keep_ref, bf16[3,64,16384]{2,1,0:T(8,128)(2,1)S(1)} %copy-done, bf16[3,64,16384]{2,1,0:T(8,128)(2,1)S(1)} %copy-done), custom_call_target="tpu_custom_call" | custom-call | flops 2097152 | bytes 6291456 | tf_op jit(solution)/shard_map/pallas_call | solution.py:266
  17.4 0.0 copy-start.1
  17.4 1.3 copy-done.1
  18.7 33.6 %all-gather.2.cloned.1.call-done.earlier_ref.taps_ref = bf16[4096,128]{1,0:T(8,128)(2,1)} async-done(((bf16[512,128]{1,0:T(8,128)(2,1)}), bf16[4096,128]{1,0:T(8,128)(2,1)}) %all-gather.2.cloned.1.call-update) | async-done | bytes 1048592 | tf_op jit(solution)/shard_map/all_gather | solution.py:404
  52.4 3.5 %all-to-all-start.1 = ((bf16[32,2,128,128]{3,2,1,0:T(8,128)(2,1)}), bf16[32,2,128,128]{3,2,1,0:T(8,128)(2,1)}, u32[]{:S(2)}, u32[]{:S(2)}) async-start(bf16[32,2,128,128]{3,2,1,0:T(8,128)(2,1)} %shard_map.146), calls=%async_computation.1 | async-start | bytes 4194304 | tf_op jit(solution)/shard_map/all_to_all | solution.py:406
  55.9 0.0 copy-start.14
  55.9 0.0 copy-start.2
  55.9 0.0 copy-start.3
  55.9 0.0 copy-start.7
  55.9 0.0 copy-start.8
  55.9 0.0 copy-start.10
  55.9 0.0 copy-start.11
  55.9 0.0 copy-start.13
  56.0 3.2 %slice.3 = bf16[1,64,16384]{2,1,0:T(8,128)(2,1)} slice(bf16[3,64,16384]{2,1,0:T(8,128)(2,1)} %value_ref.1), slice={[0:1], [0:64], [0:16384]} | slice | bytes 4194304 | tf_op jit(solution)/shard_map/slice | solution.py:408
  59.1 0.0 copy-done.14
  59.1 0.1 dynamic_slice.7.gain_ref
  59.2 0.0 copy-done.2
  59.2 0.0 copy-done.3
  59.2 0.0 copy-done.8
  59.3 22.1 %shard_map.147.spectrum_ref = f32[2,8192,128]{2,1,0:T(8,128)} custom-call(bf16[4096,128]{1,0:T(8,128)(2,1)S(1)} %copy-done.2, bf16[256,128]{1,0:T(8,128)(2,1)S(1)} %copy-done.13, f32[2,128,128]{2,1,0:T(8,128)S(1)} %copy-done.7, f32[2,128,128]{2,1,0:T(8,128)S(1)} %copy-done.8, bf16[128,192]{1,0:T(8,128)(2,1)S(1)} %copy-done.10, ...), custom_call_target="tpu_custom_call" | custom-call | flops 10000000000 | bytes 16777216 | tf_op jit(solution)/shard_map/pallas_call | solution.py:333
  81.3 23.3 %all-to-all-done.1.signal_ref = bf16[32,2,128,128]{3,2,1,0:T(8,128)(2,1)} async-done(((bf16[32,2,128,128]{3,2,1,0:T(8,128)(2,1)}), bf16[32,2,128,128]{3,2,1,0:T(8,128)(2,1)}, u32[]{:S(2)}, u32[]{:S(2)}) %all-to-all-start.1) | async-done | bytes 2097184 | tf_op jit(solution)/shard_map/all_to_all | solution.py:406
  104.6 0.0 copy-start.12
  104.6 3.8 %all-to-all-start = ((bf16[4,16,16384]{2,1,0:T(8,128)(2,1)}), bf16[4,16,16384]{2,1,0:T(8,128)(2,1)S(1)}, u32[]{:S(2)}, u32[]{:S(2)}) async-start(bf16[4,16,16384]{2,1,0:T(8,128)(2,1)} %bitcast.4), calls=%async_computation | async-start | bytes 4194304 | tf_op jit(solution)/shard_map/all_to_all | solution.py:407
  108.4 46.9 %shard_map.148 = bf16[8,2,512,128]{3,2,1,0:T(8,128)(2,1)} custom-call(bf16[32,2,128,128]{3,2,1,0:T(8,128)(2,1)} %all-to-all-done.1.signal_ref, f32[2,8192,128]{2,1,0:T(8,128)} %shard_map.147.spectrum_ref, f32[2]{0:T(128)S(1)} %dynamic_slice.7.gain_ref, bf16[256,256]{1,0:T(8,128)(2,1)S(1)} %copy-done.9, bf16[128,768]{1,0:T(8,128)(2,1)S(1)} %copy-done.6, ...), custom_call_target="tpu_custom_call" | custom-call | flops 20000000000 | bytes 16777216 | tf_op jit(solution)/shard_map/pallas_call | solution.py:333
  155.4 0.0 all-to-all-done.gate_ref
  155.4 52.6 %all_to_all.15.summed_ref = bf16[8,2,512,128]{3,2,1,0:T(8,128)(2,1)S(1)} all-to-all(bf16[8,2,512,128]{3,2,1,0:T(8,128)(2,1)} %shard_map.148), channel_id=1, replica_groups=mesh['seq'=8,'chan'=4] {'seq'}, dimensions={0} | all-to-all | bytes 4194304 | tf_op jit(solution)/shard_map/all_to_all | solution.py:414
  208.0 4.4 %shard_map.149 = bf16[16,65536]{1,0:T(8,128)(2,1)} custom-call(bf16[4,16,16384]{2,1,0:T(8,128)(2,1)S(1)} %all-to-all-done.gate_ref, bf16[8,2,512,128]{3,2,1,0:T(8,128)(2,1)S(1)} %all_to_all.15.summed_ref), custom_call_target="tpu_custom_call" | custom-call | flops 2097152 | bytes 6291456 | tf_op jit(solution)/shard_map/pallas_call | solution.py:314
  (15 shorter events, 0.0 us)
Async XLA Ops:
  6.5 45.8 %all-gather.2.cloned.1.call-start = ((), (), s32[]{:S(2)}) async-start(), calls=%async_computation.3 | async-start | bytes 1179648 | tf_op jit(solution)/shard_map/all_gather | solution.py:404
  9.6 2.8 %copy-start = (bf16[3,64,16384]{2,1,0:T(8,128)(2,1)S(1)}, bf16[3,64,16384]{2,1,0:T(8,128)(2,1)}, u32[]{:S(2)}) copy-start(bf16[3,64,16384]{2,1,0:T(8,128)(2,1)} %value_ref.1) | copy-start | bytes 18874372
  17.4 1.3 copy-start.1
  52.4 52.2 %all-to-all-start.1 = ((bf16[32,2,128,128]{3,2,1,0:T(8,128)(2,1)}), bf16[32,2,128,128]{3,2,1,0:T(8,128)(2,1)}, u32[]{:S(2)}, u32[]{:S(2)}) async-start(bf16[32,2,128,128]{3,2,1,0:T(8,128)(2,1)} %shard_map.146), calls=%async_computation.1 | async-start | bytes 4194304 | tf_op jit(solution)/shard_map/all_to_all | solution.py:406
  55.9 3.3 %copy-start.14 = (f32[16]{0:T(128)S(1)}, f32[16]{0:T(128)}, u32[]{:S(2)}) copy-start(f32[16]{0:T(128)} %param.18) | copy-start | bytes 196
  55.9 3.3 %copy-start.2 = (bf16[4096,128]{1,0:T(8,128)(2,1)S(1)}, bf16[4096,128]{1,0:T(8,128)(2,1)}, u32[]{:S(2)}) copy-start(bf16[4096,128]{1,0:T(8,128)(2,1)} %all-gather.2.cloned.1.call-done.earlier_ref.taps_ref) | copy-start | bytes 3145732
  55.9 3.3 %copy-start.3 = (bf16[768,256]{1,0:T(8,128)(2,1)S(1)}, bf16[768,256]{1,0:T(8,128)(2,1)}, u32[]{:S(2)}) copy-start(bf16[768,256]{1,0:T(8,128)(2,1)} %constant.57.clone.third_ref) | copy-start | bytes 1179652
  55.9 3.3 %copy-start.7 = (f32[2,128,128]{2,1,0:T(8,128)S(1)}, f32[2,128,128]{2,1,0:T(8,128)}, u32[]{:S(2)}) copy-start(f32[2,128,128]{2,1,0:T(8,128)} %constant.60.clone.start_ref) | copy-start | bytes 393220
  55.9 3.3 %copy-start.8 = (f32[2,128,128]{2,1,0:T(8,128)S(1)}, f32[2,128,128]{2,1,0:T(8,128)}, u32[]{:S(2)}) copy-start(f32[2,128,128]{2,1,0:T(8,128)} %constant.61.clone.step_ref) | copy-start | bytes 393220
  55.9 3.3 %copy-start.10 = (bf16[128,192]{1,0:T(8,128)(2,1)S(1)}, bf16[128,192]{1,0:T(8,128)(2,1)}, u32[]{:S(2)}) copy-start(bf16[128,192]{1,0:T(8,128)(2,1)} %constant.55.clone.second_ref) | copy-start | bytes 147460
  55.9 3.3 %copy-start.11 = (f32[2,64,128]{2,1,0:T(8,128)S(1)}, f32[2,64,128]{2,1,0:T(8,128)}, u32[]{:S(2)}) copy-start(f32[2,64,128]{2,1,0:T(8,128)} %constant.62.clone.outer_ref) | copy-start | bytes 196612
  55.9 3.3 %copy-start.13 = (bf16[256,128]{1,0:T(8,128)(2,1)S(1)}, bf16[256,128]{1,0:T(8,128)(2,1)}, u32[]{:S(2)}) copy-start(bf16[256,128]{1,0:T(8,128)(2,1)} %constant.53.clone.mat_ref) | copy-start | bytes 196612
  104.6 3.8 %copy-start.4 = (bf16[512,256]{1,0:T(8,128)(2,1)S(1)}, bf16[512,256]{1,0:T(8,128)(2,1)}, u32[]{:S(2)}) copy-start(bf16[512,256]{1,0:T(8,128)(2,1)} %constant.58.clone.third_ref) | copy-start | bytes 786436
  104.6 3.8 %copy-start.5 = (bf16[512,256]{1,0:T(8,128)(2,1)S(1)}, bf16[512,256]{1,0:T(8,128)(2,1)}, u32[]{:S(2)}) copy-start(bf16[512,256]{1,0:T(8,128)(2,1)} %constant.59.clone.third_back_ref) | copy-start | bytes 786436
  104.6 3.8 %copy-start.6 = (bf16[128,768]{1,0:T(8,128)(2,1)S(1)}, bf16[128,768]{1,0:T(8,128)(2,1)}, u32[]{:S(2)}) copy-start(bf16[128,768]{1,0:T(8,128)(2,1)} %constant.54.clone.last_ref) | copy-start | bytes 589828
  104.6 3.8 %copy-start.9 = (bf16[256,256]{1,0:T(8,128)(2,1)S(1)}, bf16[256,256]{1,0:T(8,128)(2,1)}, u32[]{:S(2)}) copy-start(bf16[256,256]{1,0:T(8,128)(2,1)} %constant.52.clone.mat_ref) | copy-start | bytes 393220
  104.6 3.8 %copy-start.12 = (bf16[128,192]{1,0:T(8,128)(2,1)S(1)}, bf16[128,192]{1,0:T(8,128)(2,1)}, u32[]{:S(2)}) copy-start(bf16[128,192]{1,0:T(8,128)(2,1)} %constant.56.clone.back_ref) | copy-start | bytes 147460
  104.6 50.7 %all-to-all-start = ((bf16[4,16,16384]{2,1,0:T(8,128)(2,1)}), bf16[4,16,16384]{2,1,0:T(8,128)(2,1)S(1)}, u32[]{:S(2)}, u32[]{:S(2)}) async-start(bf16[4,16,16384]{2,1,0:T(8,128)(2,1)} %bitcast.4), calls=%async_computation | async-start | bytes 4194304 | tf_op jit(solution)/shard_map/all_to_all | solution.py:407
Sparse Core Ops, SparseCore 0:
  9.5 42.8 all-gather.1

commit v5 on v4

--- a/solution.py
+++ b/solution.py
@@ -74,8 +74,8 @@
     return jnp.dot(a, b, preferred_element_type=jnp.float32)
 
 
-WIDE = 8
-ROWS = 8
+WIDE = 16
+ROWS = 16
 
 
 def columns(step):
@@ -153,7 +153,8 @@
 
 
 def signal_kernel(
-    signal_ref,
+    even_ref,
+    odd_ref,
     spectrum_ref,
     gain_ref,
     mat_ref,
@@ -169,13 +170,13 @@
     held,
     wide,
 ):
-    sources, _, rows, _ = signal_ref.shape
+    sources, rows, _ = even_ref.shape
     targets, _, span, _ = out_ref.shape
 
     def widen(step, carry):
         where = pl.ds(pl.multiple_of(step * rows, rows), rows)
-        for part in range(2):
-            wide[part, where, :] = signal_ref[step, part].astype(jnp.float32)
+        wide[0, where, :] = even_ref[step].astype(jnp.float32)
+        wide[1, where, :] = odd_ref[step].astype(jnp.float32)
         return carry
 
     lax.fori_loop(0, sources, widen, 0)
@@ -238,8 +239,8 @@
     lax.fori_loop(0, targets, narrow, 0)
 
 
-def product_kernel(keep_ref, key_ref, value_ref, out_ref, wide):
-    pairs, _, _, sub, _ = out_ref.shape
+def product_kernel(keep_ref, key_ref, value_ref, even_ref, odd_ref, wide):
+    pairs, _, sub, _ = even_ref.shape
     rows = 2 * pairs
 
     def one(step, carry):
@@ -253,7 +254,8 @@
 
     lax.fori_loop(0, sub // 8, one, 0)
     for row in range(rows):
-        out_ref[row // 2, 0, row % 2] = wide[row * sub : (row + 1) * sub, :].astype(jnp.bfloat16)
+        out_ref = odd_ref if row % 2 else even_ref
+        out_ref[row // 2, 0] = wide[row * sub : (row + 1) * sub, :].astype(jnp.bfloat16)
 
 
 def multiply(keep, projected, chan, pairs):
@@ -266,9 +268,9 @@
     return pl.pallas_call(
         product_kernel,
         grid=(chan,),
-        out_shape=jax.ShapeDtypeStruct((pairs, chan, 2, sub, R), jnp.bfloat16),
+        out_shape=[jax.ShapeDtypeStruct((pairs, chan, sub, R), jnp.bfloat16)] * 2,
         in_specs=[pl.BlockSpec(memory_space=pltpu.SMEM), rows_of(1), rows_of(2)],
-        out_specs=pl.BlockSpec((pairs, 1, 2, sub, R), lambda at: (0, at, 0, 0, 0)),
+        out_specs=[pl.BlockSpec((pairs, 1, sub, R), lambda at: (0, at, 0, 0))] * 2,
         scratch_shapes=[pltpu.VMEM((2 * pairs * sub, R), jnp.float32)],
         compiler_params=pltpu.CompilerParams(vmem_limit_bytes=24 * 1024 * 1024),
         cost_estimate=pl.CostEstimate(
@@ -360,7 +362,7 @@
     )
 
 
-def convolve(signal, spectrum, gain, targets, tabs):
+def convolve(even, odd, spectrum, gain, targets, tabs):
     names = (
         "first",
         "last",
@@ -379,8 +381,9 @@
         jnp.bfloat16,
         2 * 10**10,
         (2, HALF * Q, R),
-        (2,),
-        signal,
+        (3,),
+        even,
+        odd,
         spectrum,
         gain,
         *operands,
@@ -397,20 +400,22 @@
     sub = live_blocks.shape[0] // chan
     span = here * chan
     keep = lax.dynamic_slice_in_dim(live_blocks, at_chan * sub, sub)
-    rows = multiply(keep, projected, chan, pairs)
-    rows = jnp.repeat(rows, copies, axis=0) if copies > 1 else rows
-    rows = rows.reshape(seq * chan, 2, here // R, R)
+    halves_of = multiply(keep, projected, chan, pairs)
+    if copies > 1:
+        halves_of = [jnp.repeat(rows, copies, axis=0) for rows in halves_of]
+    even, odd = [rows.reshape(seq * chan, here // R, R) for rows in halves_of]
     taps = filters.astype(jnp.bfloat16).reshape(span // R, R)
     taps = lax.all_gather(taps, "seq", axis=0, tiled=True)
-    rows = follow(rows, taps)
-    rows = lax.all_to_all(rows, ("seq", "chan"), split_axis=0, concat_axis=0, tiled=True)
+    odd = follow(odd, taps)
+    even = lax.all_to_all(even, ("seq", "chan"), split_axis=0, concat_axis=0, tiled=True)
+    odd = lax.all_to_all(odd, ("seq", "chan"), split_axis=0, concat_axis=0, tiled=True)
     gate = lax.all_to_all(
         projected[0].reshape(chan, own, here), "chan", split_axis=0, concat_axis=0, tiled=True
     )
     tabs = {name: jnp.asarray(table) for name, table in tables().items()}
     spectrum = transform_taps(taps, tabs)
     gain = lax.dynamic_slice_in_dim(skip_gain, 2 * (at_seq // copies), 2)
-    summed = convolve(rows, spectrum, gain, seq, tabs)
+    summed = convolve(even, odd, spectrum, gain, seq, tabs)
     summed = lax.all_to_all(summed, "seq", split_axis=0, concat_axis=0, tiled=True)
     return apply_gate(gate, summed[::copies])
 

time: 220 us -> 214 us (0.973)
  waiting for transfers between devices: 56.9 us -> 47.8 us
  starting transfers between devices: 7.25 us -> 14.4 us
  Pallas kernels: 78.4 us -> 74.1 us
    all_to_all x1 -> x2, waiting for transfers between devices: 23.3 us -> 2.23 us  [the longest x1 2.22 us: body(): lax.all_to_all(odd, ('seq', 'chan'), split_axis=0, concat_axis=0, tiled=T...]
    all_gather x1, waiting for transfers between devices: 33.6 us -> 45.5 us  [body(): taps = lax.all_gather(taps, 'seq', axis=0, tiled=True)]
    all_to_all x1 -> x2, starting transfers between devices: 3.49 us -> 10.7 us  [the longest x1 7.3 us: body(): lax.all_to_all(even, ('seq', 'chan'), split_axis=0, concat_axis=0, tiled=...]
    pallas_call x2, Pallas kernels: 69 us -> 64 us  [run(): pl.pallas_call(kernel, out_shape=jax.ShapeDtypeStruct(out_shape, out_dtyp...]
    unnamed x30 -> x36, local copies, waits for them, and re-layouts: 4.19 us -> 5.93 us
  transfers between devices with their start and end apart: 3 -> 4, of which waited for: 2 -> 2; matrix products, arithmetic and copies ran while one was open for 2% -> 2% of each run, Pallas kernels for 34% -> 30%
where the time goes in v5:
time: 214 us
  Pallas kernels  74.1 us (35%)
  blocking collectives  52.6 us (25%)
  waiting for transfers between devices  47.8 us (22%)
  starting transfers between devices  14.4 us (7%)
  between operations  13.6 us (6%)
  local copies, waits for them, and re-layouts  9.92 us (5%)
    pallas_call x2, Pallas kernels, run(): pl.pallas_call(kernel, out_shape=jax.ShapeDtypeStruct(out_shape, out_dtyp...  64 us
    all_to_all x1, blocking collectives, body(): lax.all_to_all(summed, 'seq', split_axis=0, concat_axis=0, tiled=True)  52.6 us
    all_gather x1, waiting for transfers between devices, body(): taps = lax.all_gather(taps, 'seq', axis=0, tiled=True)  45.5 us
    all_to_all x1, starting transfers between devices, body(): lax.all_to_all(even, ('seq', 'chan'), split_axis=0, concat_axis=0, tiled=...  7.3 us
    unnamed x36, local copies, waits for them, and re-layouts  5.93 us
    pallas_call x1, Pallas kernels, multiply(): pl.pallas_call(product_kernel, grid=(chan,), out_shape=[jax.ShapeDtypeStr...  5.63 us
    pallas_call x1, Pallas kernels, apply_gate(): pl.pallas_call(gate_kernel, grid=(chan,), out_shape=jax.ShapeDtypeStruct(...  4.41 us
  transfers between devices with their start and end apart: 4, of which 2 were waited for; matrix products, arithmetic and copies ran while one was open for 2% of the time, Pallas kernels for 30%

profile of v5, /device:TPU:0, one launch (start us, length us, event | category | flops | bytes accessed | tf_op | source)
XLA Modules:
  0.0 213.7 jit_solution(4108322289150294128)
XLA Ops:
  6.5 0.8 dynamic_slice.6.keep_ref
  7.3 2.8 %copy-done = bf16[3,64,16384]{2,1,0:T(8,128)(2,1)S(1)} copy-done((bf16[3,64,16384]{2,1,0:T(8,128)(2,1)S(1)}, bf16[3,64,16384]{2,1,0:T(8,128)(2,1)}, u32[]{:S(2)}) %copy-start) | copy-done | bytes 6291480
  10.1 5.6 %shard_map.145 = (bf16[8,4,128,128]{3,2,1,0:T(8,128)(2,1)}, bf16[8,4,128,128]{3,2,1,0:T(8,128)(2,1)S(1)}) custom-call(s32[128]{0:T(128)S(1)} %dynamic_slice.6.keep_ref, bf16[3,64,16384]{2,1,0:T(8,128)(2,1)S(1)} %copy-done, bf16[3,64,16384]{2,1,0:T(8,128)(2,1)S(1)} %copy-done), custom_call_target="tpu_custom_call" | custom-call | flops 2097152 | bytes 6291456 | tf_op jit(solution)/shard_map/pallas_call | solution.py:268
  15.7 1.1 copy-done.1
  16.8 7.3 %all-to-all-start.1 = ((bf16[32,128,128]{2,1,0:T(8,128)(2,1)}), bf16[32,128,128]{2,1,0:T(8,128)(2,1)S(1)}, u32[]{:S(2)}, u32[]{:S(2)}) async-start(bf16[32,128,128]{2,1,0:T(8,128)(2,1)} %bitcast.1), calls=%async_computation.1 | async-start | bytes 2097152 | tf_op jit(solution)/shard_map/all_to_all | solution.py:410
  24.1 0.0 all-gather.2.cloned.1.call-start
  24.1 1.3 convert_reduce_fusion
  25.5 0.0 all-gather.2.cloned.1.call-update
  25.5 45.5 %all-gather.2.cloned.1.call-done.earlier_ref.taps_ref = bf16[4096,128]{1,0:T(8,128)(2,1)} async-done(((bf16[512,128]{1,0:T(8,128)(2,1)}), bf16[4096,128]{1,0:T(8,128)(2,1)}) %all-gather.2.cloned.1.call-update) | async-done | bytes 1048592 | tf_op jit(solution)/shard_map/all_gather | solution.py:408
  71.0 0.0 all-to-all-done.1.even_ref
  71.0 1.0 copy-done.14
  72.0 3.4 %all-to-all-start.2 = ((bf16[32,128,128]{2,1,0:T(8,128)(2,1)}), bf16[32,128,128]{2,1,0:T(8,128)(2,1)S(1)}, u32[]{:S(2)}, u32[]{:S(2)}) async-start(bf16[32,128,128]{2,1,0:T(8,128)(2,1)} %shard_map.146), calls=%async_computation.2 | async-start | bytes 2097152 | tf_op jit(solution)/shard_map/all_to_all | solution.py:411
  75.4 0.0 copy-start.17
  75.4 0.0 copy-start.3
  75.4 0.0 copy-start.7
  75.4 0.0 copy-start.8
  75.4 0.0 copy-start.10
  75.5 0.0 copy-start.11
  75.5 0.0 copy-start.13
  75.5 3.2 %slice.3 = bf16[1,64,16384]{2,1,0:T(8,128)(2,1)} slice(bf16[3,64,16384]{2,1,0:T(8,128)(2,1)} %value_ref.1), slice={[0:1], [0:64], [0:16384]} | slice | bytes 4194304 | tf_op jit(solution)/shard_map/slice | solution.py:413
  78.7 0.0 copy-done.17
  78.7 0.1 dynamic_slice.7.gain_ref
  78.7 0.0 copy-done.2
  78.8 20.6 %shard_map.147.spectrum_ref = f32[2,8192,128]{2,1,0:T(8,128)} custom-call(bf16[4096,128]{1,0:T(8,128)(2,1)S(1)} %copy-done.2, bf16[256,128]{1,0:T(8,128)(2,1)S(1)} %copy-done.13, f32[2,128,128]{2,1,0:T(8,128)S(1)} %copy-done.7, f32[2,128,128]{2,1,0:T(8,128)S(1)} %copy-done.8, bf16[128,192]{1,0:T(8,128)(2,1)S(1)} %copy-done.10, ...), custom_call_target="tpu_custom_call" | custom-call | flops 10000000000 | bytes 16777216 | tf_op jit(solution)/shard_map/pallas_call | solution.py:335
  99.4 2.2 %all-to-all-done.2.odd_ref = bf16[32,128,128]{2,1,0:T(8,128)(2,1)S(1)} async-done(((bf16[32,128,128]{2,1,0:T(8,128)(2,1)}), bf16[32,128,128]{2,1,0:T(8,128)(2,1)S(1)}, u32[]{:S(2)}, u32[]{:S(2)}) %all-to-all-start.2) | async-done | bytes 1048608 | tf_op jit(solution)/shard_map/all_to_all | solution.py:411
  101.6 1.0 copy-done.15
  102.6 0.0 copy-start.12
  102.6 3.8 %all-to-all-start = ((bf16[4,16,16384]{2,1,0:T(8,128)(2,1)}), bf16[4,16,16384]{2,1,0:T(8,128)(2,1)S(1)}, u32[]{:S(2)}, u32[]{:S(2)}) async-start(bf16[4,16,16384]{2,1,0:T(8,128)(2,1)} %bitcast.5), calls=%async_computation | async-start | bytes 4194304 | tf_op jit(solution)/shard_map/all_to_all | solution.py:412
  106.5 43.4 %shard_map.148 = bf16[8,2,512,128]{3,2,1,0:T(8,128)(2,1)} custom-call(bf16[32,128,128]{2,1,0:T(8,128)(2,1)} %copy-done.14, bf16[32,128,128]{2,1,0:T(8,128)(2,1)} %copy-done.15, f32[2,8192,128]{2,1,0:T(8,128)} %shard_map.147.spectrum_ref, f32[2]{0:T(128)S(1)} %dynamic_slice.7.gain_ref, bf16[256,256]{1,0:T(8,128)(2,1)S(1)} %copy-done.9, ...), custom_call_target="tpu_custom_call" | custom-call | flops 20000000000 | bytes 16777216 | tf_op jit(solution)/shard_map/pallas_call | solution.py:335
  149.9 0.0 all-to-all-done.gate_ref
  149.9 52.6 %all_to_all.20.summed_ref = bf16[8,2,512,128]{3,2,1,0:T(8,128)(2,1)S(1)} all-to-all(bf16[8,2,512,128]{3,2,1,0:T(8,128)(2,1)} %shard_map.148), channel_id=1, replica_groups=mesh['seq'=8,'chan'=4] {'seq'}, dimensions={0} | all-to-all | bytes 4194304 | tf_op jit(solution)/shard_map/all_to_all | solution.py:419
  202.5 4.4 %shard_map.149 = bf16[16,65536]{1,0:T(8,128)(2,1)} custom-call(bf16[4,16,16384]{2,1,0:T(8,128)(2,1)S(1)} %all-to-all-done.gate_ref, bf16[8,2,512,128]{3,2,1,0:T(8,128)(2,1)S(1)} %all_to_all.20.summed_ref), custom_call_target="tpu_custom_call" | custom-call | flops 2097152 | bytes 6291456 | tf_op jit(solution)/shard_map/pallas_call | solution.py:316
  (23 shorter events, 0.0 us)
Async XLA Ops:
  7.3 2.8 %copy-start = (bf16[3,64,16384]{2,1,0:T(8,128)(2,1)S(1)}, bf16[3,64,16384]{2,1,0:T(8,128)(2,1)}, u32[]{:S(2)}) copy-start(bf16[3,64,16384]{2,1,0:T(8,128)(2,1)} %value_ref.1) | copy-start | bytes 18874372
  15.7 1.1 copy-start.1
  16.8 7.4 %copy-start.16 = (f32[1,65536]{1,0:T(1,128)S(1)}, f32[1,65536]{1,0:T(1,128)}, u32[]{:S(2)}) copy-start(f32[1,65536]{1,0:T(1,128)} %param.17) | copy-start | bytes 786436
  16.8 54.2 %all-to-all-start.1 = ((bf16[32,128,128]{2,1,0:T(8,128)(2,1)}), bf16[32,128,128]{2,1,0:T(8,128)(2,1)S(1)}, u32[]{:S(2)}, u32[]{:S(2)}) async-start(bf16[32,128,128]{2,1,0:T(8,128)(2,1)} %bitcast.1), calls=%async_computation.1 | async-start | bytes 2097152 | tf_op jit(solution)/shard_map/all_to_all | solution.py:410
  24.1 46.9 %all-gather.2.cloned.1.call-start = ((), (), s32[]{:S(2)}) async-start(), calls=%async_computation.4 | async-start | bytes 1179648 | tf_op jit(solution)/shard_map/all_gather | solution.py:408
  71.0 1.0 copy-start.14
  72.0 29.6 %all-to-all-start.2 = ((bf16[32,128,128]{2,1,0:T(8,128)(2,1)}), bf16[32,128,128]{2,1,0:T(8,128)(2,1)S(1)}, u32[]{:S(2)}, u32[]{:S(2)}) async-start(bf16[32,128,128]{2,1,0:T(8,128)(2,1)} %shard_map.146), calls=%async_computation.2 | async-start | bytes 2097152 | tf_op jit(solution)/shard_map/all_to_all | solution.py:411
  75.4 3.3 %copy-start.17 = (f32[16]{0:T(128)S(1)}, f32[16]{0:T(128)}, u32[]{:S(2)}) copy-start(f32[16]{0:T(128)} %param.18) | copy-start | bytes 196
  75.4 3.3 %copy-start.2 = (bf16[4096,128]{1,0:T(8,128)(2,1)S(1)}, bf16[4096,128]{1,0:T(8,128)(2,1)}, u32[]{:S(2)}) copy-start(bf16[4096,128]{1,0:T(8,128)(2,1)} %all-gather.2.cloned.1.call-done.earlier_ref.taps_ref) | copy-start | bytes 3145732
  75.4 3.3 %copy-start.3 = (bf16[768,256]{1,0:T(8,128)(2,1)S(1)}, bf16[768,256]{1,0:T(8,128)(2,1)}, u32[]{:S(2)}) copy-start(bf16[768,256]{1,0:T(8,128)(2,1)} %constant.57.clone.third_ref) | copy-start | bytes 1179652
  75.4 3.3 %copy-start.7 = (f32[2,128,128]{2,1,0:T(8,128)S(1)}, f32[2,128,128]{2,1,0:T(8,128)}, u32[]{:S(2)}) copy-start(f32[2,128,128]{2,1,0:T(8,128)} %constant.60.clone.start_ref) | copy-start | bytes 393220
  75.4 3.3 %copy-start.8 = (f32[2,128,128]{2,1,0:T(8,128)S(1)}, f32[2,128,128]{2,1,0:T(8,128)}, u32[]{:S(2)}) copy-start(f32[2,128,128]{2,1,0:T(8,128)} %constant.61.clone.step_ref) | copy-start | bytes 393220
  75.4 3.3 %copy-start.10 = (bf16[128,192]{1,0:T(8,128)(2,1)S(1)}, bf16[128,192]{1,0:T(8,128)(2,1)}, u32[]{:S(2)}) copy-start(bf16[128,192]{1,0:T(8,128)(2,1)} %constant.55.clone.second_ref) | copy-start | bytes 147460
  75.5 3.3 %copy-start.11 = (f32[2,64,128]{2,1,0:T(8,128)S(1)}, f32[2,64,128]{2,1,0:T(8,128)}, u32[]{:S(2)}) copy-start(f32[2,64,128]{2,1,0:T(8,128)} %constant.62.clone.outer_ref) | copy-start | bytes 196612
  75.5 3.3 %copy-start.13 = (bf16[256,128]{1,0:T(8,128)(2,1)S(1)}, bf16[256,128]{1,0:T(8,128)(2,1)}, u32[]{:S(2)}) copy-start(bf16[256,128]{1,0:T(8,128)(2,1)} %constant.53.clone.mat_ref) | copy-start | bytes 196612
  101.6 1.0 copy-start.15
  102.6 3.8 %copy-start.4 = (bf16[512,256]{1,0:T(8,128)(2,1)S(1)}, bf16[512,256]{1,0:T(8,128)(2,1)}, u32[]{:S(2)}) copy-start(bf16[512,256]{1,0:T(8,128)(2,1)} %constant.58.clone.third_ref) | copy-start | bytes 786436
  102.6 3.8 %copy-start.5 = (bf16[512,256]{1,0:T(8,128)(2,1)S(1)}, bf16[512,256]{1,0:T(8,128)(2,1)}, u32[]{:S(2)}) copy-start(bf16[512,256]{1,0:T(8,128)(2,1)} %constant.59.clone.third_back_ref) | copy-start | bytes 786436
  102.6 3.8 %copy-start.6 = (bf16[128,768]{1,0:T(8,128)(2,1)S(1)}, bf16[128,768]{1,0:T(8,128)(2,1)}, u32[]{:S(2)}) copy-start(bf16[128,768]{1,0:T(8,128)(2,1)} %constant.54.clone.last_ref) | copy-start | bytes 589828
  102.6 3.8 %copy-start.9 = (bf16[256,256]{1,0:T(8,128)(2,1)S(1)}, bf16[256,256]{1,0:T(8,128)(2,1)}, u32[]{:S(2)}) copy-start(bf16[256,256]{1,0:T(8,128)(2,1)} %constant.52.clone.mat_ref) | copy-start | bytes 393220
  102.6 3.8 %copy-start.12 = (bf16[128,192]{1,0:T(8,128)(2,1)S(1)}, bf16[128,192]{1,0:T(8,128)(2,1)}, u32[]{:S(2)}) copy-start(bf16[128,192]{1,0:T(8,128)(2,1)} %constant.56.clone.back_ref) | copy-start | bytes 147460
  102.6 47.2 %all-to-all-start = ((bf16[4,16,16384]{2,1,0:T(8,128)(2,1)}), bf16[4,16,16384]{2,1,0:T(8,128)(2,1)S(1)}, u32[]{:S(2)}, u32[]{:S(2)}) async-start(bf16[4,16,16384]{2,1,0:T(8,128)(2,1)} %bitcast.5), calls=%async_computation | async-start | bytes 4194304 | tf_op jit(solution)/shard_map/all_to_all | solution.py:412
Sparse Core Ops, SparseCore 0:
  27.1 43.9 all-gather.1

commit v6 on v5

--- a/solution.py
+++ b/solution.py
@@ -239,8 +239,8 @@
     lax.fori_loop(0, targets, narrow, 0)
 
 
-def product_kernel(keep_ref, key_ref, value_ref, even_ref, odd_ref, wide):
-    pairs, _, sub, _ = even_ref.shape
+def product_kernel(keep_ref, key_ref, value_ref, _, even_ref, odd_ref, wide):
+    pairs, sub = even_ref.shape[0], even_ref.shape[2]
     rows = 2 * pairs
 
     def one(step, carry):
@@ -258,7 +258,7 @@
         out_ref[row // 2, 0] = wide[row * sub : (row + 1) * sub, :].astype(jnp.bfloat16)
 
 
-def multiply(keep, projected, chan, pairs):
+def multiply(keep, projected, earlier, chan, pairs):
     sub = keep.shape[0]
     here = sub * R
 
@@ -269,28 +269,33 @@
         product_kernel,
         grid=(chan,),
         out_shape=[jax.ShapeDtypeStruct((pairs, chan, sub, R), jnp.bfloat16)] * 2,
-        in_specs=[pl.BlockSpec(memory_space=pltpu.SMEM), rows_of(1), rows_of(2)],
+        in_specs=[
+            pl.BlockSpec(memory_space=pltpu.SMEM),
+            rows_of(1),
+            rows_of(2),
+            pl.BlockSpec(memory_space=pl.ANY),
+        ],
         out_specs=[pl.BlockSpec((pairs, 1, sub, R), lambda at: (0, at, 0, 0))] * 2,
         scratch_shapes=[pltpu.VMEM((2 * pairs * sub, R), jnp.float32)],
         compiler_params=pltpu.CompilerParams(vmem_limit_bytes=24 * 1024 * 1024),
         cost_estimate=pl.CostEstimate(
             flops=4 * chan * pairs * here, bytes_accessed=12 * chan * pairs * here, transcendentals=0
         ),
-    )(keep, projected, projected)
-
-
-def follow_kernel(value_ref, earlier_ref, out_ref):
-    del value_ref, earlier_ref, out_ref
-
-
-def follow(value, earlier):
+    )(keep, projected, projected, earlier)
+
+
+def follow_kernel(*refs):
+    del refs
+
+
+def follow(value, *earlier):
     return pl.pallas_call(
         follow_kernel,
         out_shape=jax.ShapeDtypeStruct(value.shape, value.dtype),
-        in_specs=[pl.BlockSpec(memory_space=pl.ANY)] * 2,
+        in_specs=[pl.BlockSpec(memory_space=pl.ANY)] * (1 + len(earlier)),
         out_specs=pl.BlockSpec(memory_space=pl.ANY),
         input_output_aliases={0: 0},
-    )(value, earlier)
+    )(value, *earlier)
 
 
 def gate_kernel(gate_ref, summed_ref, out_ref, wide):
@@ -400,18 +405,18 @@
     sub = live_blocks.shape[0] // chan
     span = here * chan
     keep = lax.dynamic_slice_in_dim(live_blocks, at_chan * sub, sub)
-    halves_of = multiply(keep, projected, chan, pairs)
+    taps = filters.astype(jnp.bfloat16).reshape(span // R, R)
+    halves_of = multiply(keep, projected, taps, chan, pairs)
     if copies > 1:
         halves_of = [jnp.repeat(rows, copies, axis=0) for rows in halves_of]
     even, odd = [rows.reshape(seq * chan, here // R, R) for rows in halves_of]
-    taps = filters.astype(jnp.bfloat16).reshape(span // R, R)
     taps = lax.all_gather(taps, "seq", axis=0, tiled=True)
-    odd = follow(odd, taps)
-    even = lax.all_to_all(even, ("seq", "chan"), split_axis=0, concat_axis=0, tiled=True)
-    odd = lax.all_to_all(odd, ("seq", "chan"), split_axis=0, concat_axis=0, tiled=True)
     gate = lax.all_to_all(
         projected[0].reshape(chan, own, here), "chan", split_axis=0, concat_axis=0, tiled=True
     )
+    odd = follow(odd, taps, gate)
+    even = lax.all_to_all(even, ("seq", "chan"), split_axis=0, concat_axis=0, tiled=True)
+    odd = lax.all_to_all(odd, ("seq", "chan"), split_axis=0, concat_axis=0, tiled=True)
     tabs = {name: jnp.asarray(table) for name, table in tables().items()}
     spectrum = transform_taps(taps, tabs)
     gain = lax.dynamic_slice_in_dim(skip_gain, 2 * (at_seq // copies), 2)

time: 214 us -> 230 us (1.075)
  waiting for transfers between devices: 47.8 us -> 66.9 us
    all_to_all x1, waiting for transfers between devices: 0.01 us -> 14.7 us  [body(): lax.all_to_all(projected[0].reshape(chan, own, here), 'chan', split_axis=...]
    all_to_all x1, waiting for transfers between devices: 2.22 us -> 5.35 us  [body(): lax.all_to_all(odd, ('seq', 'chan'), split_axis=0, concat_axis=0, tiled=T...]
    unnamed x36 -> x40, local copies, waits for them, and re-layouts: 5.93 us -> 3.99 us
  transfers between devices with their start and end apart: 4 -> 4, of which waited for: 2 -> 3; matrix products, arithmetic and copies ran while one was open for 2% -> 1% of each run, Pallas kernels for 30% -> 11%
where the time goes in v6:
time: 230 us; the launch traced here: 229 us
  Pallas kernels  74.2 us (32%)
  waiting for transfers between devices  66.9 us (29%)
  blocking collectives  52.1 us (23%)
  starting transfers between devices  13.7 us (6%)
  between operations  13.6 us (6%)
  local copies, waits for them, and re-layouts  7.87 us (3%)
    pallas_call x2, Pallas kernels, run(): pl.pallas_call(kernel, out_shape=jax.ShapeDtypeStruct(out_shape, out_dtyp...  64.2 us
    all_to_all x1, blocking collectives, body(): lax.all_to_all(summed, 'seq', split_axis=0, concat_axis=0, tiled=True)  52.1 us
    all_gather x1, waiting for transfers between devices, body(): taps = lax.all_gather(taps, 'seq', axis=0, tiled=True)  46.2 us
    all_to_all x1, waiting for transfers between devices, body(): lax.all_to_all(projected[0].reshape(chan, own, here), 'chan', split_axis=...  14.7 us
    all_to_all x1, starting transfers between devices, body(): lax.all_to_all(even, ('seq', 'chan'), split_axis=0, concat_axis=0, tiled=...  5.69 us
    pallas_call x1, Pallas kernels, multiply(): pl.pallas_call(product_kernel, grid=(chan,), out_shape=[jax.ShapeDtypeStr...  5.63 us
    all_to_all x1, waiting for transfers between devices, body(): lax.all_to_all(odd, ('seq', 'chan'), split_axis=0, concat_axis=0, tiled=T...  5.35 us
  transfers between devices with their start and end apart: 4, of which 3 were waited for; matrix products, arithmetic and copies ran while one was open for 1% of the time, Pallas kernels for 11%

profile of v6, /device:TPU:0, one launch (start us, length us, event | category | flops | bytes accessed | tf_op | source)
XLA Modules:
  0.0 229.2 jit_solution(13629524330646005595)
XLA Ops:
  6.5 3.0 %slice.3 = bf16[1,64,16384]{2,1,0:T(8,128)(2,1)} slice(bf16[3,64,16384]{2,1,0:T(8,128)(2,1)} %value_ref.1), slice={[0:1], [0:64], [0:16384]} | slice | bytes 4194304 | tf_op jit(solution)/shard_map/slice | solution.py:415
  9.6 4.4 %all-to-all-start = ((bf16[4,16,16384]{2,1,0:T(8,128)(2,1)}), bf16[4,16,16384]{2,1,0:T(8,128)(2,1)S(1)}, u32[]{:S(2)}, u32[]{:S(2)}) async-start(bf16[4,16,16384]{2,1,0:T(8,128)(2,1)} %bitcast.7), calls=%async_computation | async-start | bytes 4194304 | tf_op jit(solution)/shard_map/all_to_all | solution.py:414
  13.9 0.8 dynamic_slice.6.keep_ref
  14.7 0.7 convert_reduce_fusion
  15.4 0.0 copy-start
  15.4 2.8 %copy-done = bf16[3,64,16384]{2,1,0:T(8,128)(2,1)S(1)} copy-done((bf16[3,64,16384]{2,1,0:T(8,128)(2,1)S(1)}, bf16[3,64,16384]{2,1,0:T(8,128)(2,1)}, u32[]{:S(2)}) %copy-start) | copy-done | bytes 6291480
  18.2 5.6 %shard_map.145 = (bf16[8,4,128,128]{3,2,1,0:T(8,128)(2,1)}, bf16[8,4,128,128]{3,2,1,0:T(8,128)(2,1)S(1)}) custom-call(s32[128]{0:T(128)S(1)} %dynamic_slice.6.keep_ref, bf16[3,64,16384]{2,1,0:T(8,128)(2,1)S(1)} %copy-done, bf16[3,64,16384]{2,1,0:T(8,128)(2,1)S(1)} %copy-done, bf16[512,128]{1,0:T(8,128)(2,1)S(1)} %bitcast.5), custom_call_target="tpu_custom_call" | custom-call | flops 2097152 | bytes 6291456 | tf_op jit(solution)/shard_map/pallas_call | solution.py:268
  23.9 1.1 copy-done.3
  24.9 14.7 %all-to-all-done.refs_2_.gate_ref = bf16[4,16,16384]{2,1,0:T(8,128)(2,1)S(1)} async-done(((bf16[4,16,16384]{2,1,0:T(8,128)(2,1)}), bf16[4,16,16384]{2,1,0:T(8,128)(2,1)S(1)}, u32[]{:S(2)}, u32[]{:S(2)}) %all-to-all-start) | async-done | bytes 2097184 | tf_op jit(solution)/shard_map/all_to_all | solution.py:414
  39.7 5.7 %all-to-all-start.1 = ((bf16[32,128,128]{2,1,0:T(8,128)(2,1)}), bf16[32,128,128]{2,1,0:T(8,128)(2,1)S(1)}, u32[]{:S(2)}, u32[]{:S(2)}) async-start(bf16[32,128,128]{2,1,0:T(8,128)(2,1)} %bitcast.1), calls=%async_computation.1 | async-start | bytes 2097152 | tf_op jit(solution)/shard_map/all_to_all | solution.py:418
  45.3 0.0 all-gather.2.cloned.1.call-start
  45.4 0.7 all-gather.2.cloned.1.call-update
  46.1 46.2 %all-gather.2.cloned.1.call-done.refs_1_.taps_ref = bf16[4096,128]{1,0:T(8,128)(2,1)} async-done(((bf16[512,128]{1,0:T(8,128)(2,1)}), bf16[4096,128]{1,0:T(8,128)(2,1)}) %all-gather.2.cloned.1.call-update) | async-done | bytes 1048592 | tf_op jit(solution)/shard_map/all_gather | solution.py:413
  92.3 0.0 copy-start.10
  92.3 0.0 copy-start.11
  92.3 0.0 copy-start.13
  92.3 0.0 copy-start.14
  92.3 0.0 copy-start.16
  92.4 0.0 all-to-all-done.1.even_ref
  92.4 3.6 %all-to-all-start.2 = ((bf16[32,128,128]{2,1,0:T(8,128)(2,1)}), bf16[32,128,128]{2,1,0:T(8,128)(2,1)}, u32[]{:S(2)}, u32[]{:S(2)}) async-start(bf16[32,128,128]{2,1,0:T(8,128)(2,1)} %shard_map.146), calls=%async_computation.2 | async-start | bytes 2097152 | tf_op jit(solution)/shard_map/all_to_all | solution.py:419
  96.0 0.1 dynamic_slice.7.gain_ref
  96.1 0.0 copy-done.5
  96.1 0.0 copy-start.7
  96.2 0.0 copy-start.8
  96.2 0.0 copy-start.9
  96.2 0.0 copy-start.12
  96.2 0.0 copy-start.15
  96.2 20.6 %shard_map.147.spectrum_ref = f32[2,8192,128]{2,1,0:T(8,128)} custom-call(bf16[4096,128]{1,0:T(8,128)(2,1)S(1)} %copy-done.5, bf16[256,128]{1,0:T(8,128)(2,1)S(1)} %copy-done.16, f32[2,128,128]{2,1,0:T(8,128)S(1)} %copy-done.11, f32[2,128,128]{2,1,0:T(8,128)S(1)} %copy-done.10, bf16[128,192]{1,0:T(8,128)(2,1)S(1)} %copy-done.14, ...), custom_call_target="tpu_custom_call" | custom-call | flops 10000000000 | bytes 16777216 | tf_op jit(solution)/shard_map/pallas_call | solution.py:340
  116.8 5.3 %all-to-all-done.2.odd_ref = bf16[32,128,128]{2,1,0:T(8,128)(2,1)} async-done(((bf16[32,128,128]{2,1,0:T(8,128)(2,1)}), bf16[32,128,128]{2,1,0:T(8,128)(2,1)}, u32[]{:S(2)}, u32[]{:S(2)}) %all-to-all-start.2) | async-done | bytes 1048608 | tf_op jit(solution)/shard_map/all_to_all | solution.py:419
  122.2 43.6 %shard_map.148 = bf16[8,2,512,128]{3,2,1,0:T(8,128)(2,1)} custom-call(bf16[32,128,128]{2,1,0:T(8,128)(2,1)} %copy-done.17, bf16[32,128,128]{2,1,0:T(8,128)(2,1)} %all-to-all-done.2.odd_ref, f32[2,8192,128]{2,1,0:T(8,128)} %shard_map.147.spectrum_ref, f32[2]{0:T(128)S(1)} %dynamic_slice.7.gain_ref, bf16[256,256]{1,0:T(8,128)(2,1)S(1)} %copy-done.12, ...), custom_call_target="tpu_custom_call" | custom-call | flops 20000000000 | bytes 16777216 | tf_op jit(solution)/shard_map/pallas_call | solution.py:340
  165.8 52.1 %all_to_all.20.summed_ref = bf16[8,2,512,128]{3,2,1,0:T(8,128)(2,1)S(1)} all-to-all(bf16[8,2,512,128]{3,2,1,0:T(8,128)(2,1)} %shard_map.148), channel_id=1, replica_groups=mesh['seq'=8,'chan'=4] {'seq'}, dimensions={0} | all-to-all | bytes 4194304 | tf_op jit(solution)/shard_map/all_to_all | solution.py:424
  217.9 4.4 %shard_map.149 = bf16[16,65536]{1,0:T(8,128)(2,1)} custom-call(bf16[4,16,16384]{2,1,0:T(8,128)(2,1)S(1)} %copy-done.2, bf16[8,2,512,128]{3,2,1,0:T(8,128)(2,1)S(1)} %all_to_all.20.summed_ref), custom_call_target="tpu_custom_call" | custom-call | flops 2097152 | bytes 6291456 | tf_op jit(solution)/shard_map/pallas_call | solution.py:321
  (27 shorter events, 0.1 us)
Async XLA Ops:
  9.6 5.1 %copy-start.18 = (f32[1,65536]{1,0:T(1,128)S(1)}, f32[1,65536]{1,0:T(1,128)}, u32[]{:S(2)}) copy-start(f32[1,65536]{1,0:T(1,128)} %param.17) | copy-start | bytes 786436
  9.6 30.1 %all-to-all-start = ((bf16[4,16,16384]{2,1,0:T(8,128)(2,1)}), bf16[4,16,16384]{2,1,0:T(8,128)(2,1)S(1)}, u32[]{:S(2)}, u32[]{:S(2)}) async-start(bf16[4,16,16384]{2,1,0:T(8,128)(2,1)} %bitcast.7), calls=%async_computation | async-start | bytes 4194304 | tf_op jit(solution)/shard_map/all_to_all | solution.py:414
  15.4 8.5 %copy-start.4 = (bf16[65536]{0:T(1024)(128)(2,1)}, bf16[65536]{0:T(1024)(128)(2,1)S(1)}, u32[]{:S(2)}) copy-start(bf16[65536]{0:T(1024)(128)(2,1)S(1)} %convert_reduce_fusion) | copy-start | bytes 393220
  15.4 2.8 %copy-start = (bf16[3,64,16384]{2,1,0:T(8,128)(2,1)S(1)}, bf16[3,64,16384]{2,1,0:T(8,128)(2,1)}, u32[]{:S(2)}) copy-start(bf16[3,64,16384]{2,1,0:T(8,128)(2,1)} %value_ref.1) | copy-start | bytes 18874372
  23.9 1.1 copy-start.3
  39.6 52.6 %copy-start.1 = (bf16[4,16,16384]{2,1,0:T(8,128)(2,1)}, bf16[4,16,16384]{2,1,0:T(8,128)(2,1)S(1)}, u32[]{:S(2)}) copy-start(bf16[4,16,16384]{2,1,0:T(8,128)(2,1)S(1)} %all-to-all-done.refs_2_.gate_ref) | copy-start | bytes 6291460
  39.7 52.7 %all-to-all-start.1 = ((bf16[32,128,128]{2,1,0:T(8,128)(2,1)}), bf16[32,128,128]{2,1,0:T(8,128)(2,1)S(1)}, u32[]{:S(2)}, u32[]{:S(2)}) async-start(bf16[32,128,128]{2,1,0:T(8,128)(2,1)} %bitcast.1), calls=%async_computation.1 | async-start | bytes 2097152 | tf_op jit(solution)/shard_map/all_to_all | solution.py:418
  45.3 46.9 %all-gather.2.cloned.1.call-start = ((), (), s32[]{:S(2)}) async-start(), calls=%async_computation.4 | async-start | bytes 1179648 | tf_op jit(solution)/shard_map/all_gather | solution.py:413
  92.3 3.7 %copy-start.19 = (f32[16]{0:T(128)S(1)}, f32[16]{0:T(128)}, u32[]{:S(2)}) copy-start(f32[16]{0:T(128)} %param.18) | copy-start | bytes 196
  92.3 3.8 %copy-start.5 = (bf16[4096,128]{1,0:T(8,128)(2,1)S(1)}, bf16[4096,128]{1,0:T(8,128)(2,1)}, u32[]{:S(2)}) copy-start(bf16[4096,128]{1,0:T(8,128)(2,1)} %all-gather.2.cloned.1.call-done.refs_1_.taps_ref) | copy-start | bytes 3145732
  92.3 3.8 %copy-start.6 = (bf16[768,256]{1,0:T(8,128)(2,1)S(1)}, bf16[768,256]{1,0:T(8,128)(2,1)}, u32[]{:S(2)}) copy-start(bf16[768,256]{1,0:T(8,128)(2,1)} %constant.57.clone.third_ref) | copy-start | bytes 1179652
  92.3 3.8 %copy-start.10 = (f32[2,128,128]{2,1,0:T(8,128)S(1)}, f32[2,128,128]{2,1,0:T(8,128)}, u32[]{:S(2)}) copy-start(f32[2,128,128]{2,1,0:T(8,128)} %constant.61.clone.step_ref) | copy-start | bytes 393220
  92.3 3.8 %copy-start.11 = (f32[2,128,128]{2,1,0:T(8,128)S(1)}, f32[2,128,128]{2,1,0:T(8,128)}, u32[]{:S(2)}) copy-start(f32[2,128,128]{2,1,0:T(8,128)} %constant.60.clone.start_ref) | copy-start | bytes 393220
  92.3 3.8 %copy-start.13 = (f32[2,64,128]{2,1,0:T(8,128)S(1)}, f32[2,64,128]{2,1,0:T(8,128)}, u32[]{:S(2)}) copy-start(f32[2,64,128]{2,1,0:T(8,128)} %constant.62.clone.outer_ref) | copy-start | bytes 196612
  92.3 3.8 %copy-start.14 = (bf16[128,192]{1,0:T(8,128)(2,1)S(1)}, bf16[128,192]{1,0:T(8,128)(2,1)}, u32[]{:S(2)}) copy-start(bf16[128,192]{1,0:T(8,128)(2,1)} %constant.55.clone.second_ref) | copy-start | bytes 147460
  92.3 3.8 %copy-start.16 = (bf16[256,128]{1,0:T(8,128)(2,1)S(1)}, bf16[256,128]{1,0:T(8,128)(2,1)}, u32[]{:S(2)}) copy-start(bf16[256,128]{1,0:T(8,128)(2,1)} %constant.53.clone.mat_ref) | copy-start | bytes 196612
  92.4 3.6 %copy-start.17 = (bf16[32,128,128]{2,1,0:T(8,128)(2,1)}, bf16[32,128,128]{2,1,0:T(8,128)(2,1)S(1)}, u32[]{:S(2)}) copy-start(bf16[32,128,128]{2,1,0:T(8,128)(2,1)S(1)} %all-to-all-done.1.even_ref) | copy-start | bytes 3145732
  92.4 29.8 %all-to-all-start.2 = ((bf16[32,128,128]{2,1,0:T(8,128)(2,1)}), bf16[32,128,128]{2,1,0:T(8,128)(2,1)}, u32[]{:S(2)}, u32[]{:S(2)}) async-start(bf16[32,128,128]{2,1,0:T(8,128)(2,1)} %shard_map.146), calls=%async_computation.2 | async-start | bytes 2097152 | tf_op jit(solution)/shard_map/all_to_all | solution.py:419
  96.1 26.0 %copy-start.7 = (bf16[512,256]{1,0:T(8,128)(2,1)S(1)}, bf16[512,256]{1,0:T(8,128)(2,1)}, u32[]{:S(2)}) copy-start(bf16[512,256]{1,0:T(8,128)(2,1)} %constant.59.clone.third_back_ref) | copy-start | bytes 786436
  96.2 26.0 %copy-start.8 = (bf16[512,256]{1,0:T(8,128)(2,1)S(1)}, bf16[512,256]{1,0:T(8,128)(2,1)}, u32[]{:S(2)}) copy-start(bf16[512,256]{1,0:T(8,128)(2,1)} %constant.58.clone.third_ref) | copy-start | bytes 786436
  96.2 26.0 %copy-start.9 = (bf16[128,768]{1,0:T(8,128)(2,1)S(1)}, bf16[128,768]{1,0:T(8,128)(2,1)}, u32[]{:S(2)}) copy-start(bf16[128,768]{1,0:T(8,128)(2,1)} %constant.54.clone.last_ref) | copy-start | bytes 589828
  96.2 26.0 %copy-start.12 = (bf16[256,256]{1,0:T(8,128)(2,1)S(1)}, bf16[256,256]{1,0:T(8,128)(2,1)}, u32[]{:S(2)}) copy-start(bf16[256,256]{1,0:T(8,128)(2,1)} %constant.52.clone.mat_ref) | copy-start | bytes 393220
  96.2 26.0 %copy-start.15 = (bf16[128,192]{1,0:T(8,128)(2,1)S(1)}, bf16[128,192]{1,0:T(8,128)(2,1)}, u32[]{:S(2)}) copy-start(bf16[128,192]{1,0:T(8,128)(2,1)} %constant.56.clone.back_ref) | copy-start | bytes 147460
  165.8 52.1 %copy-start.2 = (bf16[4,16,16384]{2,1,0:T(8,128)(2,1)S(1)}, bf16[4,16,16384]{2,1,0:T(8,128)(2,1)}, u32[]{:S(2)}) copy-start(bf16[4,16,16384]{2,1,0:T(8,128)(2,1)} %copy-done.1) | copy-start | bytes 6291460
Sparse Core Ops, SparseCore 0:
  48.3 43.9 all-gather.1
